TPU v7x, 256 devices: a whole 4x4x8 slice. The times are simulated.
256 devices in a mesh: rows: 32 (over x, y, core), feat: 8 (over z).
Axes of the slice: x: 4, y: 4, z: 8, core: 2. Of those that a mesh axis runs over, the one named last changes fastest.
Arguments:
- fact_table: bfloat16 [65536, 1024], P('rows', 'feat'), may hold values from -6 to 6
- dim_table: bfloat16 [131072, 1024], P('rows', 'feat'), may hold values from -6 to 6
- fact_weight: float32 [1024], P('feat'), may hold values from -0.125 to 0.125
- dim_weight: float32 [1024], P('feat'), may hold values from -0.125 to 0.125
- bucket: int32 [65536, 1], P('rows'), may hold values from 0 to 31; in each aligned block of 2048 rows (0 to 2047, 2048 to 4095, ...) at most 128 rows name the same one
- row_index: int32 [65536], P('rows'), may hold values from 0 to 4095
- labels: int32 [65536], P('rows'), may hold values 0 or 1
Outputs:
- new_fact_weight: float32 [1024], P('feat')
- new_dim_weight: float32 [1024], P('feat')
- fact_prob: float32 [65536], P('rows')
Inputs may be any that keep to these rules, and one draw needn't show every extreme that they name: `bucket`: among the rows of one device no owner is named by more than 128 rows, a bound that some block reaches.
All inputs are finite; a program needn't handle non-finite values. No bound on the sum of `labels` on one device may be relied on, other than what follows from the above.
Results may differ from a plain program's by a relative error of at most 0.0003.
Values may be sent and summed in bfloat16 or wider, within the bound.
No kernel may reach another device: no remote copies, remote signals or barrier semaphores. Data moves between devices by JAX's collectives and lax.ppermute only.
A program may use at most 64 MiB of HBM per device.

v0:
```python
import math

import jax
import jax.numpy as jnp
from jax import lax
from jax.sharding import PartitionSpec as P


def by_blocks(total, blockfn):
    block = math.gcd(total, 512)
    starts = jnp.arange(total // block, dtype=jnp.int32) * block
    pieces = lax.map(lambda start: blockfn(start, block), starts)
    return pieces.reshape((total,) + pieces.shape[2:])


def shards(fact_table, dim_table, fact_weight, dim_weight, bucket, row_index, labels):
    peer_count = lax.axis_size("rows")
    rows_here = fact_table.shape[0]
    dim_here = dim_table.shape[0]
    capacity = 2 * rows_here // peer_count
    slot_total = peer_count * capacity
    dest_owner = bucket[:, 0]
    route_hits = (dest_owner[:, None] == jnp.arange(peer_count, dtype=jnp.int32)[None, :]).astype(
        jnp.int32
    )
    slot_index = jnp.sum((jnp.cumsum(route_hits, 0) - 1) * route_hits, 1)
    flat_dest = dest_owner * capacity + slot_index
    labels_real = labels.astype(jnp.float32)
    grad_scale = 1.0 / jnp.sqrt(jnp.float32(rows_here * peer_count))

    def place_rows(values):

        def packer(start, block):
            slot_ids = start + jnp.arange(block, dtype=jnp.int32)
            hit = slot_ids[:, None] == flat_dest[None, :]
            if values.ndim == 2:
                return jnp.dot(
                    hit.astype(values.dtype), values, preferred_element_type=jnp.float32
                ).astype(values.dtype)
            return jnp.sum(jnp.where(hit, values[None, :], jnp.zeros((), values.dtype)), 1)

        packed = by_blocks(slot_total, packer)
        return packed.reshape((peer_count, capacity) + values.shape[1:])

    recv_feat, recv_label, recv_index, recv_valid = (
        lax.all_to_all(place_rows(fact_table), "rows", split_axis=0, concat_axis=0, tiled=True),
        lax.all_to_all(
            place_rows(labels_real.astype(jnp.bfloat16)),
            "rows",
            split_axis=0,
            concat_axis=0,
            tiled=True,
        ),
        lax.all_to_all(place_rows(row_index), "rows", split_axis=0, concat_axis=0, tiled=True),
        lax.all_to_all(
            place_rows(jnp.ones((rows_here,), jnp.bfloat16)),
            "rows",
            split_axis=0,
            concat_axis=0,
            tiled=True,
        ),
    )
    flat_feat = recv_feat.reshape(-1, recv_feat.shape[-1])
    flat_index = recv_index.reshape(-1)

    def joiner(start, block):
        wanted = lax.dynamic_slice_in_dim(flat_index, start, block, 0)
        onehot = (wanted[:, None] == jnp.arange(dim_here, dtype=jnp.int32)[None, :]).astype(
            dim_table.dtype
        )
        return jnp.dot(onehot, dim_table, preferred_element_type=jnp.float32).astype(
            dim_table.dtype
        )

    joined = by_blocks(slot_total, joiner)
    partial_value = jnp.dot(
        flat_feat, fact_weight, precision=lax.Precision.HIGHEST, preferred_element_type=jnp.float32
    )
    partial_value = partial_value + jnp.dot(
        joined, dim_weight, precision=lax.Precision.HIGHEST, preferred_element_type=jnp.float32
    )
    logits = lax.psum(partial_value.reshape(peer_count, capacity), "feat")
    probability = jax.nn.sigmoid(logits)
    residual = (probability - recv_label.astype(jnp.float32)) * recv_valid.astype(jnp.float32)
    flat_resid = residual.reshape(-1)
    grad_fact = jnp.dot(
        flat_resid, flat_feat, precision=lax.Precision.HIGHEST, preferred_element_type=jnp.float32
    )
    grad_dim = jnp.dot(
        flat_resid, joined, precision=lax.Precision.HIGHEST, preferred_element_type=jnp.float32
    )
    returned = lax.all_to_all(probability, "rows", split_axis=0, concat_axis=0, tiled=True)
    fact_prob = jnp.take(returned.reshape(-1), flat_dest)
    grad_fact, grad_dim = lax.psum((grad_fact, grad_dim), "rows")
    return (
        fact_weight - 0.5 * grad_fact * grad_scale,
        dim_weight - 0.5 * grad_dim * grad_scale,
        fact_prob,
    )


def solution(mesh):
    return jax.shard_map(
        shards,
        mesh=mesh,
        in_specs=(
            P("rows", "feat"),
            P("rows", "feat"),
            P("feat"),
            P("feat"),
            P("rows", None),
            P("rows"),
            P("rows"),
        ),
        out_specs=(P("feat"), P("feat"), P("rows")),
        check_vma=False,
    )
```

profile of v0, /device:TPU:1, one launch (start us, length us, event | category | flops | bytes accessed | tf_op | source)
XLA Modules:
  0.0 273.1 jit_solution(16110724073518105166)
XLA Ops:
  1.4 9.1 %reduce-window.6 = s32[32,16,128]{2,1,0:T(8,128)S(1)} reduce-window(s32[32,16,128]{2,1,0:T(8,128)S(1)} %fusion.22, s32[]{:T(128)} %constant.108.clone.1), window={size=1x1x128 pad=0_0x0_0x127_0}, to_apply=%region_0.0 | reduce-window | flops 8323072 | bytes 524292 | tf_op jit(solution)/shard_map/reduce-window
  11.4 14.9 %while.57 = (s32[]{:T(128)}, bf16[8,512]{1,0:T(8,128)(2,1)S(1)}, s32[8]{0:T(128)S(1)}, s32[2048]{0:T(1024)S(1)}, bf16[2048]{0:T(1024)(128)(2,1)S(1)}, /*index=5*/s32[]{:T(128)}, s32[]{:T(128)}) while((s32[]{:T(128)}, bf16[8,512]{1,0:T(8,128)(2,1)S(1)}, s32[8]{0:T(128)S(1)}, s32[2048]{0:T(1024)S(1)}, bf16[2048]{0:T(1024)(128)(2,1)S(1)}, ...), condition=%wide.region_13.14_spmd, body=%wide.region_11.13_spmd.sunk | while | flops 3145730 | bytes 21601 | solution.py:12
  27.0 8.6 %all-to-all-start.2 = ((bf16[32,1,128]{2,1,0:T(2,128)(2,1)}), bf16[32,1,128]{2,1,0:T(2,128)(2,1)S(1)}, u32[]{:S(2)}, u32[]{:S(2)}) async-start(bf16[32,1,128]{2,1,0:T(2,128)(2,1)} %all_to_all.36), calls=%async_computation.2 | async-start | bytes 32768 | tf_op jit(solution)/shard_map/all_to_all | solution.py:47
  35.6 16.0 %while.55 = (s32[]{:T(128)}, s32[8,512]{1,0:T(8,128)S(1)}, s32[8]{0:T(128)S(1)}, s32[2048]{0:T(1024)S(1)}, s32[2048]{0:T(1024)S(1)}, /*index=5*/s32[]{:T(128)}, s32[]{:T(128)}) while((s32[]{:T(128)}, s32[8,512]{1,0:T(8,128)S(1)}, s32[8]{0:T(128)S(1)}, s32[2048]{0:T(1024)S(1)}, s32[2048]{0:T(1024)S(1)}, /*index=5*/s32[]{:T(128)}, ...), condition=%wide.region_7.8_spmd, body=%wide.region_5.7_spmd.sunk | while | flops 3145730 | bytes 26721 | solution.py:12
  52.7 21.2 %while.54 = (s32[]{:T(128)}, bf16[8,512,128]{2,1,0:T(8,128)(2,1)}, s32[8]{0:T(128)S(1)}, s32[2048]{0:T(1024)S(1)}, bf16[2048,128]{1,0:T(8,128)(2,1)S(1)}, /*index=5*/s32[]{:T(128)}) while((s32[]{:T(128)}, bf16[8,512,128]{2,1,0:T(8,128)(2,1)}, s32[8]{0:T(128)S(1)}, s32[2048]{0:T(1024)S(1)}, bf16[2048,128]{1,0:T(8,128)(2,1)S(1)}, ...), condition=%wide.region_4.5_spmd, body=%wide.region_3.4_spmd.sunk | while | flops 269550080 | bytes 668245 | solution.py:12
  53.9 1.4 fusion.44
  56.6 1.4 fusion.44
  59.2 1.4 fusion.44
  61.9 1.4 fusion.44
  64.6 1.4 fusion.44
  67.2 1.4 fusion.44
  69.9 1.4 fusion.44
  72.5 1.4 fusion.44
  73.9 14.9 %while.58 = (s32[]{:T(128)}, bf16[8,512]{1,0:T(8,128)(2,1)S(1)}, s32[8]{0:T(128)S(1)}, s32[2048]{0:T(1024)S(1)}, s32[]{:T(128)}, /*index=5*/s32[]{:T(128)}) while((s32[]{:T(128)}, bf16[8,512]{1,0:T(8,128)(2,1)S(1)}, s32[8]{0:T(128)S(1)}, s32[2048]{0:T(1024)S(1)}, s32[]{:T(128)}, /*index=5*/s32[]{:T(128)}) %tuple.117), condition=%wide.region_16.17_spmd, body=%wide.region_14.16_spmd.sunk | while | flops 3145730 | bytes 17497 | solution.py:12
  89.5 7.4 %all-to-all-start.1 = ((s32[32,1,128]{2,1,0:T(1,128)}), s32[32,1,128]{2,1,0:T(1,128)S(1)}, u32[]{:S(2)}, u32[]{:S(2)}) async-start(s32[32,1,128]{2,1,0:T(1,128)} %all_to_all.28), calls=%async_computation.1 | async-start | bytes 32768 | tf_op jit(solution)/shard_map/all_to_all | solution.py:54
  97.6 6.3 %all-to-all-done.1 = s32[32,1,128]{2,1,0:T(1,128)S(1)} async-done(((s32[32,1,128]{2,1,0:T(1,128)}), s32[32,1,128]{2,1,0:T(1,128)S(1)}, u32[]{:S(2)}, u32[]{:S(2)}) %all-to-all-start.1) | async-done | bytes 16416 | tf_op jit(solution)/shard_map/all_to_all | solution.py:54
  103.8 4.2 %all-to-all-start = ((bf16[32,128,128]{2,1,0:T(8,128)(2,1)}), bf16[32,128,128]{2,1,0:T(8,128)(2,1)S(1)}, u32[]{:S(2)}, u32[]{:S(2)}) async-start(bf16[32,128,128]{2,1,0:T(8,128)(2,1)} %bitcast.13), calls=%async_computation | async-start | bytes 2097152 | tf_op jit(solution)/shard_map/all_to_all | solution.py:46
  109.3 33.6 %while.56 = (s32[]{:T(128)}, bf16[8,512,128]{2,1,0:T(8,128)(2,1)S(1)}, s32[8]{0:T(128)S(1)}, s32[4096]{0:T(1024)S(1)}, bf16[4096,128]{1,0:T(8,128)(2,1)S(1)}, /*index=5*/s32[]{:T(128)}, s32[]{:T(128)}, s32[]{:T(128)}) while((s32[]{:T(128)}, bf16[8,512,128]{2,1,0:T(8,128)(2,1)S(1)}, s32[8]{0:T(128)S(1)}, s32[4096]{0:T(1024)S(1)}, ...), condition=%wide.region_9.10_spmd, body=%wide.region_8.9_spmd.sunk | while | flops 539033600 | bytes 1185931 | solution.py:12
  111.9 1.6 fusion.46
  116.1 1.6 fusion.46
  120.3 1.6 fusion.46
  124.5 1.6 fusion.46
  128.7 1.6 fusion.46
  132.9 1.6 fusion.46
  137.1 1.6 fusion.46
  141.4 1.6 fusion.46
  143.9 7.5 %all-to-all-start.3 = ((bf16[32,1,128]{2,1,0:T(2,128)(2,1)}), bf16[32,1,128]{2,1,0:T(2,128)(2,1)S(1)}, u32[]{:S(2)}, u32[]{:S(2)}) async-start(bf16[32,1,128]{2,1,0:T(2,128)(2,1)} %all_to_all.37), calls=%async_computation.3 | async-start | bytes 32768 | tf_op jit(solution)/shard_map/all_to_all | solution.py:55
  152.3 25.8 %psum.21 = f32[32,128]{1,0:T(8,128)S(1)} all-reduce(f32[32,128]{1,0:T(8,128)S(1)} %add_bitcast_fusion), channel_id=1, replica_groups=mesh['rows'=32,'feat'=8] {'feat'}, use_global_device_ids=true, to_apply=%region_10.11 | all-reduce | flops 4096 | bytes 32768 | tf_op jit(solution)/shard_map/psum | solution.py:82
  179.8 69.4 %all-reduce = (f32[128]{0:T(128)S(1)}, f32[128]{0:T(128)S(1)}) all-reduce(f32[128]{0:T(128)S(1)} %convolution_bitcast_fusion.1, f32[128]{0:T(128)S(1)} %convolution_bitcast_fusion), channel_id=1, replica_groups=mesh['rows'=32,'feat'=8] {'rows'}, use_global_device_ids=true, to_apply=%region_17.18 | all-reduce | flops 256 | bytes 2048 | tf_op jit(solution)/shard_map/psum | solution.py:94
  249.8 3.9 %all-to-all-start.4 = ((f32[32,1,128]{2,1,0:T(1,128)}), f32[32,1,128]{2,1,0:T(1,128)S(1)}, u32[]{:S(2)}, u32[]{:S(2)}) async-start(f32[32,1,128]{2,1,0:T(1,128)} %bitcast.32), calls=%async_computation.4 | async-start | bytes 32768 | tf_op jit(solution)/shard_map/all_to_all | solution.py:92
  254.2 6.5 %all-to-all-done.4 = f32[32,1,128]{2,1,0:T(1,128)S(1)} async-done(((f32[32,1,128]{2,1,0:T(1,128)}), f32[32,1,128]{2,1,0:T(1,128)S(1)}, u32[]{:S(2)}, u32[]{:S(2)}) %all-to-all-start.4) | async-done | bytes 16416 | tf_op jit(solution)/shard_map/all_to_all | solution.py:92
  260.8 11.8 %gather_fusion = f32[2048]{0:T(1024)S(1)} fusion(f32[4096]{0:T(1024)S(1)} %bitcast.94, s32[2048]{0:T(1024)S(1)} %broadcast_clamp_fusion), kind=kCustom, calls=%fused_computation | custom fusion | bytes 24576 | tf_op jit(solution)/shard_map/jit(_take)/gather | solution.py:93
  (189 shorter events, 71.3 us)
Async XLA Ops:
  0.6 10.6 %copy-start.1 = (s32[2048,1]{0,1:T(1,128)S(1)}, s32[2048,1]{0,1:T(1,128)}, u32[]{:S(2)}) copy-start(s32[2048,1]{0,1:T(1,128)} %param.21) | copy-start | bytes 24580
  1.4 9.9 %copy-start.2 = (s32[2048]{0:T(1024)S(1)}, s32[2048]{0:T(1024)}, u32[]{:S(2)}) copy-start(s32[2048]{0:T(1024)} %param.23) | copy-start | bytes 24580
  10.5 25.0 %copy-start = (s32[2048]{0:T(1024)S(1)}, s32[2048]{0:T(1024)}, u32[]{:S(2)}) copy-start(s32[2048]{0:T(1024)} %param.22) | copy-start | bytes 24580
  11.2 41.5 %copy-start.6 = (bf16[2048,128]{1,0:T(8,128)(2,1)S(1)}, bf16[2048,128]{1,0:T(8,128)(2,1)}, u32[]{:S(2)}) copy-start(bf16[2048,128]{1,0:T(8,128)(2,1)} %param.17) | copy-start | bytes 1572868
  27.0 62.6 %all-to-all-start.2 = ((bf16[32,1,128]{2,1,0:T(2,128)(2,1)}), bf16[32,1,128]{2,1,0:T(2,128)(2,1)S(1)}, u32[]{:S(2)}, u32[]{:S(2)}) async-start(bf16[32,1,128]{2,1,0:T(2,128)(2,1)} %all_to_all.36), calls=%async_computation.2 | async-start | bytes 32768 | tf_op jit(solution)/shard_map/all_to_all | solution.py:47
  89.5 14.3 %all-to-all-start.1 = ((s32[32,1,128]{2,1,0:T(1,128)}), s32[32,1,128]{2,1,0:T(1,128)S(1)}, u32[]{:S(2)}, u32[]{:S(2)}) async-start(s32[32,1,128]{2,1,0:T(1,128)} %all_to_all.28), calls=%async_computation.1 | async-start | bytes 32768 | tf_op jit(solution)/shard_map/all_to_all | solution.py:54
  103.8 40.0 %all-to-all-start = ((bf16[32,128,128]{2,1,0:T(8,128)(2,1)}), bf16[32,128,128]{2,1,0:T(8,128)(2,1)S(1)}, u32[]{:S(2)}, u32[]{:S(2)}) async-start(bf16[32,128,128]{2,1,0:T(8,128)(2,1)} %bitcast.13), calls=%async_computation | async-start | bytes 2097152 | tf_op jit(solution)/shard_map/all_to_all | solution.py:46
  108.1 1.2 copy-start.5
  109.3 33.6 %copy-start.3 = (f32[128]{0:T(128)S(1)}, f32[128]{0:T(128)}, u32[]{:S(2)}) copy-start(f32[128]{0:T(128)} %param.20) | copy-start | bytes 1540
  142.9 8.5 %copy-start.4 = (f32[128]{0:T(128)S(1)}, f32[128]{0:T(128)}, u32[]{:S(2)}) copy-start(f32[128]{0:T(128)} %param.19) | copy-start | bytes 1540
  143.9 34.3 %all-to-all-start.3 = ((bf16[32,1,128]{2,1,0:T(2,128)(2,1)}), bf16[32,1,128]{2,1,0:T(2,128)(2,1)S(1)}, u32[]{:S(2)}, u32[]{:S(2)}) async-start(bf16[32,1,128]{2,1,0:T(2,128)(2,1)} %all_to_all.37), calls=%async_computation.3 | async-start | bytes 32768 | tf_op jit(solution)/shard_map/all_to_all | solution.py:55
  249.8 11.0 %all-to-all-start.4 = ((f32[32,1,128]{2,1,0:T(1,128)}), f32[32,1,128]{2,1,0:T(1,128)S(1)}, u32[]{:S(2)}, u32[]{:S(2)}) async-start(f32[32,1,128]{2,1,0:T(1,128)} %bitcast.32), calls=%async_computation.4 | async-start | bytes 32768 | tf_op jit(solution)/shard_map/all_to_all | solution.py:92
where the time goes:
time: 274 us; the launch traced here: 273 us
  blocking collectives  95.3 us (35%)
  other arithmetic  46.9 us (17%)
  local copies, waits for them, and re-layouts  42.3 us (15%)
  starting transfers between devices  31.6 us (12%)
  matrix products  26.8 us (10%)
  loops' own time  16.4 us (6%)
  waiting for transfers between devices  12.8 us (5%)
    psum x1, blocking collectives, shards(): grad_fact, grad_dim = lax.psum((grad_fact, grad_dim), 'rows')  69.4 us
    psum x1, blocking collectives, shards(): logits = lax.psum(partial_value.reshape(peer_count, capacity), 'feat')  25.8 us
    dynamic_slice x40, local copies, waits for them, and re-layouts, by_blocks(): pieces = lax.map(lambda start: blockfn(start, block), starts)  24.1 us
    add x32, other arithmetic, packer(): slot_ids = start + jnp.arange(block, dtype=jnp.int32)  21 us
    another operation x5, loops' own time, by_blocks(): pieces = lax.map(lambda start: blockfn(start, block), starts)  16.4 us
    reduce_sum x24, other arithmetic, packer(): jnp.sum(jnp.where(hit, values[None, :], jnp.zeros((), values.dtype)), 1)  13.2 us
    dot_general x8, matrix products, joiner(): jnp.dot(onehot, dim_table, preferred_element_type=jnp.float32)  12.6 us
    gather x1, local copies, waits for them, and re-layouts, shards(): fact_prob = jnp.take(returned.reshape(-1), flat_dest)  11.8 us
  transfers between devices with their start and end apart: 5, of which 2 were waited for; matrix products, arithmetic and copies ran while one was open for 27% of the time, Pallas kernels for 0%

commit v1 on v0

v1 whole, which is shorter than its diff:
```python
import jax
import jax.numpy as jnp
from jax import lax
from jax.experimental import pallas as pl
from jax.experimental.pallas import tpu as pltpu
from jax.sharding import PartitionSpec as P

LANES = 128
OWNERS = 32
PEERS = 8
DIM_ROWS = 32
FACT_ROWS = 16
FACTS_HERE = FACT_ROWS * LANES
SCORE_ROWS = DIM_ROWS + FACT_ROWS
BLOCK_ROWS = DIM_ROWS + 2
LABEL_BIT = 12
VALID_BIT = 13

bf16 = jnp.bfloat16
f32 = jnp.float32


def split3(value):
    high = value.astype(bf16).astype(f32)
    rest = value - high
    middle = rest.astype(bf16).astype(f32)
    return high, middle, rest - middle


def stacked_row(row):
    shape = (8, row.shape[1])
    place = lax.broadcasted_iota(jnp.int32, shape, 0)
    high, middle, low = split3(row)
    return jnp.where(
        place == 0, high, jnp.where(place == 1, middle, jnp.where(place == 2, low, 0.0))
    ).astype(bf16)


def dot_nt(left, right):
    return lax.dot_general(
        left, right, (((1,), (1,)), ((), ())), preferred_element_type=f32
    )


def dot_nn(left, right):
    return jnp.dot(left, right, preferred_element_type=f32)


def hits(row, count):
    return lax.broadcasted_iota(jnp.int32, (count, row.shape[1]), 0) == row


def onehot(row, count):
    return jnp.where(hits(row, count), 1.0, 0.0).astype(bf16)


def scores_kernel(fact_ref, dim_ref, fact_weight_ref, dim_weight_ref, out_ref):
    dim_part = jnp.sum(dot_nt(stacked_row(dim_weight_ref[...]), dim_ref[...]), 0, keepdims=True)
    fact_part = jnp.sum(dot_nt(stacked_row(fact_weight_ref[...]), fact_ref[...]), 0, keepdims=True)
    for i in range(DIM_ROWS):
        out_ref[0, i : i + 1, :] = dim_part[:, i * LANES : (i + 1) * LANES]
    for i in range(FACT_ROWS):
        out_ref[0, DIM_ROWS + i : DIM_ROWS + i + 1, :] = fact_part[:, i * LANES : (i + 1) * LANES]
    for peer in range(1, PEERS):
        out_ref[peer] = out_ref[0]


def slots_kernel(bucket_ref, index_ref, label_ref, rank_ref, meta_ref):
    width = 2 * LANES
    chunks = FACTS_HERE // width
    bucket = bucket_ref[...]
    owner_hits = onehot(bucket, OWNERS)
    stack = jnp.concatenate(
        [owner_hits[:, c * width : (c + 1) * width] for c in range(chunks)], 0
    )
    upto = jnp.where(
        lax.broadcasted_iota(jnp.int32, (width, width), 0)
        <= lax.broadcasted_iota(jnp.int32, (width, width), 1),
        1.0,
        0.0,
    ).astype(bf16)
    prefix = dot_nn(stack, upto)
    before = jnp.zeros((OWNERS, 1), f32)
    for c in range(chunks):
        here = prefix[c * OWNERS : (c + 1) * OWNERS]
        mine = hits(bucket[:, c * width : (c + 1) * width], OWNERS)
        rank_ref[:, c * width : (c + 1) * width] = (
            jnp.sum(jnp.where(mine, here + before, 0.0), 0, keepdims=True).astype(jnp.int32) - 1
        )
        before = before + here[:, width - 1 : width]
    index = index_ref[...]
    low = (index & (LANES - 1)).astype(f32)
    high = ((index >> 7) + (label_ref[...] << (LABEL_BIT - 7)) + (1 << (VALID_BIT - 7))).astype(f32)
    mine = hits(bucket, OWNERS)
    fields = jnp.concatenate([jnp.where(mine, low, 0.0), jnp.where(mine, high, 0.0)], 0)
    packed = dot_nt(fields.astype(bf16), onehot(rank_ref[...], LANES))
    meta_ref[...] = packed[:OWNERS] + packed[OWNERS:] * LANES


def pack_kernel(recv_ref, bucket_ref, rank_ref, meta_ref, out_ref, dims_ref, facts_ref, left_ref):
    total = recv_ref[0]
    for peer in range(1, PEERS):
        total = total + recv_ref[peer]
    dims_ref[...] = total[:DIM_ROWS]
    for i in range(FACT_ROWS):
        cut = slice(i * LANES, (i + 1) * LANES)
        mine = hits(bucket_ref[:, cut], OWNERS)
        for part, value in enumerate(split3(total[DIM_ROWS + i : DIM_ROWS + i + 1])):
            left_ref[part * OWNERS : (part + 1) * OWNERS, cut] = jnp.where(mine, value, 0.0).astype(bf16)
    packed = dot_nt(left_ref[...], onehot(rank_ref[...], LANES))
    packed = packed[:OWNERS] + packed[OWNERS : 2 * OWNERS] + packed[2 * OWNERS :]
    facts_ref[...] = packed
    for owner in range(OWNERS):
        out_ref[owner, :DIM_ROWS, :] = total[:DIM_ROWS]
        out_ref[owner, DIM_ROWS : DIM_ROWS + 1, :] = packed[owner : owner + 1]
        out_ref[owner, DIM_ROWS + 1 : DIM_ROWS + 2, :] = meta_ref[owner : owner + 1, :]


def stacked(value):
    return jnp.concatenate(split3(value), 0).astype(bf16)


def found(parts, row):
    value = parts[:DIM_ROWS] + parts[DIM_ROWS : 2 * DIM_ROWS] + parts[2 * DIM_ROWS :]
    return jnp.sum(jnp.where(hits(row, DIM_ROWS), value, 0.0), 0, keepdims=True)


def sigmoid(value):
    return 1.0 / (1.0 + jnp.exp(-value))


def grads_kernel(
    recv_ref,
    dims_ref,
    facts_ref,
    meta_ref,
    bucket_ref,
    rank_ref,
    label_ref,
    fact_ref,
    dim_ref,
    out_ref,
    prob_ref,
    home_ref,
    own_ref,
    code_ref,
    low_ref,
    left_ref,
):
    meta = meta_ref[...].astype(jnp.int32)
    for owner in range(OWNERS):
        code = meta[owner : owner + 1]
        parts = dot_nn(stacked(recv_ref[owner, :DIM_ROWS, :]), onehot(code & (LANES - 1), LANES))
        home_ref[owner : owner + 1, :] = found(parts, (code >> 7) & (DIM_ROWS - 1))
    dims = stacked(dims_ref[...])
    for source in range(OWNERS):
        cut = slice(source * LANES, (source + 1) * LANES)
        code = recv_ref[source, DIM_ROWS + 1 : DIM_ROWS + 2, :].astype(jnp.int32)
        code_ref[source : source + 1, :] = code
        column = onehot(code & (LANES - 1), LANES)
        low_ref[:, cut] = column
        own_ref[source : source + 1, :] = recv_ref[source, DIM_ROWS : DIM_ROWS + 1, :] + found(
            dot_nn(dims, column), (code >> 7) & (DIM_ROWS - 1)
        )
    prob = sigmoid(home_ref[...] + facts_ref[...])
    parts = dot_nn(stacked(prob), onehot(rank_ref[...], LANES))
    prob = found(parts, bucket_ref[...])
    prob_ref[...] = prob
    residual = prob - label_ref[...].astype(f32)
    grad_fact = jnp.sum(dot_nn(stacked_row(residual), fact_ref[...]), 0, keepdims=True)
    code = code_ref[...]
    residual = (sigmoid(own_ref[...]) - ((code >> LABEL_BIT) & 1).astype(f32)) * (
        code >> VALID_BIT
    ).astype(f32)
    terms = split3(residual)
    for source in range(OWNERS):
        cut = slice(source * LANES, (source + 1) * LANES)
        mine = hits((code[source : source + 1] >> 7) & (DIM_ROWS - 1), DIM_ROWS)
        for part, value in enumerate(terms):
            left_ref[part * DIM_ROWS : (part + 1) * DIM_ROWS, cut] = jnp.where(
                mine, value[source : source + 1], 0.0
            ).astype(bf16)
    sums = dot_nt(left_ref[...], low_ref[...])
    sums = sums[:DIM_ROWS] + sums[DIM_ROWS : 2 * DIM_ROWS] + sums[2 * DIM_ROWS :]
    rows = jnp.concatenate([stacked_row(sums[i : i + 1]) for i in range(DIM_ROWS)], 1)
    grad_dim = jnp.sum(dot_nn(rows, dim_ref[...]), 0, keepdims=True)
    for owner in range(OWNERS):
        out_ref[owner, 0:1, :] = grad_fact
        out_ref[owner, 1:2, :] = grad_dim


def update_kernel(recv_ref, fact_weight_ref, dim_weight_ref, fact_out_ref, dim_out_ref):
    total = recv_ref[0]
    for peer in range(1, OWNERS):
        total = total + recv_ref[peer]
    scale = 0.5 / (OWNERS * FACTS_HERE) ** 0.5
    fact_out_ref[...] = fact_weight_ref[...] - scale * total[0:1]
    dim_out_ref[...] = dim_weight_ref[...] - scale * total[1:2]


def call(kernel, outs, scratch=()):
    return pl.pallas_call(
        kernel,
        out_shape=[jax.ShapeDtypeStruct(shape, dtype) for shape, dtype in outs],
        scratch_shapes=[pltpu.VMEM(shape, dtype) for shape, dtype in scratch],
        compiler_params=pltpu.CompilerParams(vmem_limit_bytes=32 * 1024 * 1024),
    )


def exchange(value, axis):
    return lax.all_to_all(value, axis, split_axis=0, concat_axis=0, tiled=True)


def shards(fact_table, dim_table, fact_weight, dim_weight, bucket, row_index, labels):
    bucket = bucket.reshape(1, FACTS_HERE)
    row_index = row_index.reshape(1, FACTS_HERE)
    labels = labels.reshape(1, FACTS_HERE)
    fact_weight = fact_weight.reshape(1, LANES)
    dim_weight = dim_weight.reshape(1, LANES)

    (partial,) = call(scores_kernel, [((PEERS, SCORE_ROWS, LANES), f32)])(
        fact_table, dim_table, fact_weight, dim_weight
    )
    rank, meta = call(
        slots_kernel, [((1, FACTS_HERE), jnp.int32), ((OWNERS, LANES), f32)]
    )(bucket, row_index, labels)
    partial = exchange(partial, "feat")
    blocks, dims, facts = call(
        pack_kernel,
        [((OWNERS, BLOCK_ROWS, LANES), f32), ((DIM_ROWS, LANES), f32), ((OWNERS, LANES), f32)],
        [((3 * OWNERS, FACTS_HERE), bf16)],
    )(partial, bucket, rank, meta)
    blocks = exchange(blocks, "rows")
    grads, prob = call(
        grads_kernel,
        [((OWNERS, 2, LANES), f32), ((1, FACTS_HERE), f32)],
        [
            ((OWNERS, LANES), f32),
            ((OWNERS, LANES), f32),
            ((OWNERS, LANES), jnp.int32),
            ((LANES, OWNERS * LANES), bf16),
            ((3 * DIM_ROWS, OWNERS * LANES), bf16),
        ],
    )(blocks, dims, facts, meta, bucket, rank, labels, fact_table, dim_table)
    grads = exchange(grads, "rows")
    new_fact, new_dim = call(update_kernel, [((1, LANES), f32), ((1, LANES), f32)])(
        grads, fact_weight, dim_weight
    )
    return new_fact.reshape(-1), new_dim.reshape(-1), prob.reshape(-1)


def solution(mesh):
    return jax.shard_map(
        shards,
        mesh=mesh,
        in_specs=(
            P("rows", "feat"),
            P("rows", "feat"),
            P("feat"),
            P("feat"),
            P("rows", None),
            P("rows"),
            P("rows"),
        ),
        out_specs=(P("feat"), P("feat"), P("rows")),
        check_vma=False,
    )
```

time: 274 us -> 60.3 us (0.22)
  blocking collectives: 95.3 us -> 33.3 us
  other arithmetic: 46.9 us -> 0 us
  local copies, waits for them, and re-layouts: 42.3 us -> 2.94 us
  matrix products: 26.8 us -> 0 us
  starting transfers between devices: 31.6 us -> 9.15 us
  loops' own time: 16.4 us -> 0 us
  Pallas kernels: 0 us -> 5.56 us
  waiting for transfers between devices: 12.8 us -> 8.18 us
    psum x2 -> x0, blocking collectives: 95.3 us -> none  [the longest x1 69.4 us: shards(): grad_fact, grad_dim = lax.psum((grad_fact, grad_dim), 'rows')]
    all_to_all x0 -> x2, blocking collectives: none -> 33.3 us  [exchange(): return lax.all_to_all(value, axis, split_axis=0, concat_axis=0, tiled=True)]
    dot_general x20 -> x0, matrix products: 26.8 us -> none  [the longest x8 12.6 us: joiner(): jnp.dot(onehot, dim_table, preferred_element_type=jnp.float32)]
    dynamic_slice x48 -> x0, local copies, waits for them, and re-layouts: 24.7 us -> none  [the longest x40 24.1 us: by_blocks(): pieces = lax.map(lambda start: blockfn(start, block), starts)]
    all_to_all x5 -> x1, starting transfers between devices: 31.6 us -> 9.15 us  [exchange(): return lax.all_to_all(value, axis, split_axis=0, concat_axis=0, tiled=True)]
    add x32 -> x0, other arithmetic: 21 us -> none  [packer(): slot_ids = start + jnp.arange(block, dtype=jnp.int32)]
    another operation x5 -> x0, loops' own time: 16.4 us -> none  [by_blocks(): pieces = lax.map(lambda start: blockfn(start, block), starts)]
    reduce_sum x25 -> x0, other arithmetic: 13.3 us -> none  [the longest x24 13.2 us: packer(): jnp.sum(jnp.where(hit, values[None, :], jnp.zeros((), values.dtype)), 1)]
  transfers between devices with their start and end apart: 5 -> 1, of which waited for: 2 -> 1; matrix products, arithmetic and copies ran while one was open for 27% -> 0% of each run, Pallas kernels for 0% -> 1%
where the time goes in v1:
time: 60.3 us; the launch traced here: 59.9 us
  blocking collectives  33.3 us (55%)
  starting transfers between devices  9.15 us (15%)
  waiting for transfers between devices  8.18 us (14%)
  Pallas kernels  5.56 us (9%)
  local copies, waits for them, and re-layouts  2.94 us (5%)
  between operations  0.71 us (1%)
    all_to_all x2, blocking collectives, exchange(): return lax.all_to_all(value, axis, split_axis=0, concat_axis=0, tiled=True)  33.3 us
    all_to_all x1, starting transfers between devices, exchange(): return lax.all_to_all(value, axis, split_axis=0, concat_axis=0, tiled=True)  9.15 us
    all_to_all x1, waiting for transfers between devices, exchange(): return lax.all_to_all(value, axis, split_axis=0, concat_axis=0, tiled=True)  8.18 us
    unnamed x18, local copies, waits for them, and re-layouts  2.94 us
    pallas_call x1, Pallas kernels, shards(): call(grads_kernel, [((OWNERS, 2, LANES), f32), ((1, FACTS_HERE), f32)], [...  2.8 us
    pallas_call x1, Pallas kernels, shards(): call(scores_kernel, [((PEERS, SCORE_ROWS, LANES), f32)])  1.23 us
  transfers between devices with their start and end apart: 1, of which 1 were waited for; matrix products, arithmetic and copies ran while one was open for 0% of the time, Pallas kernels for 1%

profile of v1, /device:TPU:1, one launch (start us, length us, event | category | flops | bytes accessed | tf_op | source)
XLA Modules:
  0.0 59.9 jit_solution(8616549093991618663)
XLA Ops:
  0.6 0.0 copy-start.7
  0.6 0.0 copy-start.8
  0.7 0.6 %copy-done.7 = f32[128]{0:T(128)S(1)} copy-done((f32[128]{0:T(128)S(1)}, f32[128]{0:T(128)}, u32[]{:S(2)}) %copy-start.7) | copy-done | bytes 536
  1.3 0.0 copy-done.8
  1.3 0.0 copy-start
  1.3 1.2 %copy-done = bf16[4096,128]{1,0:T(8,128)(2,1)S(1)} copy-done((bf16[4096,128]{1,0:T(8,128)(2,1)S(1)}, bf16[4096,128]{1,0:T(8,128)(2,1)}, u32[]{:S(2)}) %copy-start) | copy-done | bytes 1048600
  2.5 0.0 copy-start.2
  2.5 1.0 %copy-done.2 = bf16[2048,128]{1,0:T(8,128)(2,1)S(1)} copy-done((bf16[2048,128]{1,0:T(8,128)(2,1)S(1)}, bf16[2048,128]{1,0:T(8,128)(2,1)}, u32[]{:S(2)}) %copy-start.2) | copy-done | bytes 524312
  3.6 0.0 copy-start.4
  3.6 0.0 copy-start.5
  3.6 0.0 copy-start.6
  3.6 1.2 %shard_map.94 = f32[8,48,128]{2,1,0:T(8,128)} custom-call(bf16[2048,128]{1,0:T(8,128)(2,1)S(1)} %copy-done.2, bf16[4096,128]{1,0:T(8,128)(2,1)S(1)} %copy-done, f32[1,128]{1,0:T(1,128)S(1)} %bitcast.14, f32[1,128]{1,0:T(1,128)S(1)} %bitcast.16), custom_call_target="tpu_custom_call" | custom-call | tf_op jit(solution)/shard_map/pallas_call | solution.py:221
  4.8 0.0 copy-start.1
  4.8 9.1 %all-to-all-start = ((f32[8,48,128]{2,1,0:T(8,128)}), f32[8,48,128]{2,1,0:T(8,128)S(1)}, u32[]{:S(2)}, u32[]{:S(2)}) async-start(f32[8,48,128]{2,1,0:T(8,128)} %shard_map.94), calls=%async_computation | async-start | bytes 393216 | tf_op jit(solution)/shard_map/all_to_all | solution.py:211
  14.0 0.0 copy-done.4
  14.0 0.0 copy-done.5
  14.0 0.0 copy-done.6
  14.0 0.6 shard_map.95
  14.6 8.2 %all-to-all-done.recv_ref = f32[8,48,128]{2,1,0:T(8,128)S(1)} async-done(((f32[8,48,128]{2,1,0:T(8,128)}), f32[8,48,128]{2,1,0:T(8,128)S(1)}, u32[]{:S(2)}, u32[]{:S(2)}) %all-to-all-start) | async-done | bytes 196640 | tf_op jit(solution)/shard_map/all_to_all | solution.py:211
  22.8 0.4 shard_map.96
  23.2 0.0 copy-start.3
  23.2 22.6 %all_to_all.15.recv_ref = f32[32,34,128]{2,1,0:T(8,128)S(1)} all-to-all(f32[32,34,128]{2,1,0:T(8,128)S(1)} %get-tuple-element.14), channel_id=1, replica_groups=mesh['rows'=32,'feat'=8] {'rows'}, dimensions={0} | all-to-all | bytes 1114112 | tf_op jit(solution)/shard_map/all_to_all | solution.py:211
  45.8 0.0 copy-done.1
  45.8 0.0 copy-done.3
  45.8 2.8 %shard_map.97 = (f32[32,2,128]{2,1,0:T(2,128)S(1)}, f32[1,2048]{1,0:T(1,128)}) custom-call(f32[32,34,128]{2,1,0:T(8,128)S(1)} %all_to_all.15.recv_ref, f32[32,128]{1,0:T(8,128)S(1)} %get-tuple-element.15.dims_ref, f32[32,128]{1,0:T(8,128)S(1)} %get-tuple-element.16.facts_ref, f32[32,128]{1,0:T(8,128)S(1)} %get-tuple-element.13.meta_ref, ...), custom_call_target="tpu_custom_call" | custom-call | tf_op jit(solution)/shard_map/pallas_call | solution.py:234
  48.6 10.8 %all_to_all.16.recv_ref = f32[32,2,128]{2,1,0:T(2,128)S(1)} all-to-all(f32[32,2,128]{2,1,0:T(2,128)S(1)} %get-tuple-element.17), channel_id=1, replica_groups=mesh['rows'=32,'feat'=8] {'rows'}, dimensions={0} | all-to-all | bytes 65536 | tf_op jit(solution)/shard_map/all_to_all | solution.py:211
  59.3 0.6 shard_map.98
Async XLA Ops:
  0.6 0.7 %copy-start.7 = (f32[128]{0:T(128)S(1)}, f32[128]{0:T(128)}, u32[]{:S(2)}) copy-start(f32[128]{0:T(128)} %param.9) | copy-start | bytes 1540
  0.6 0.7 %copy-start.8 = (f32[128]{0:T(128)S(1)}, f32[128]{0:T(128)}, u32[]{:S(2)}) copy-start(f32[128]{0:T(128)} %param.10) | copy-start | bytes 1540
  1.3 1.2 %copy-start = (bf16[4096,128]{1,0:T(8,128)(2,1)S(1)}, bf16[4096,128]{1,0:T(8,128)(2,1)}, u32[]{:S(2)}) copy-start(bf16[4096,128]{1,0:T(8,128)(2,1)} %dim_ref.3) | copy-start | bytes 3145732
  2.5 1.0 %copy-start.2 = (bf16[2048,128]{1,0:T(8,128)(2,1)S(1)}, bf16[2048,128]{1,0:T(8,128)(2,1)}, u32[]{:S(2)}) copy-start(bf16[2048,128]{1,0:T(8,128)(2,1)} %fact_ref.3) | copy-start | bytes 1572868
  3.6 10.4 %copy-start.4 = (s32[2048,1]{0,1:T(1,128)S(1)}, s32[2048,1]{0,1:T(1,128)}, u32[]{:S(2)}) copy-start(s32[2048,1]{0,1:T(1,128)} %param.11) | copy-start | bytes 24580
  3.6 10.4 %copy-start.5 = (s32[2048]{0:T(1024)S(1)}, s32[2048]{0:T(1024)}, u32[]{:S(2)}) copy-start(s32[2048]{0:T(1024)} %param.13) | copy-start | bytes 24580
  3.6 10.4 %copy-start.6 = (s32[2048]{0:T(1024)S(1)}, s32[2048]{0:T(1024)}, u32[]{:S(2)}) copy-start(s32[2048]{0:T(1024)} %param.12) | copy-start | bytes 24580
  4.8 41.0 %copy-start.1 = (bf16[4096,128]{1,0:T(8,128)(2,1)S(1)}, bf16[4096,128]{1,0:T(8,128)(2,1)}, u32[]{:S(2)}) copy-start(bf16[4096,128]{1,0:T(8,128)(2,1)} %dim_ref.3) | copy-start | bytes 3145732
  4.8 18.0 %all-to-all-start = ((f32[8,48,128]{2,1,0:T(8,128)}), f32[8,48,128]{2,1,0:T(8,128)S(1)}, u32[]{:S(2)}, u32[]{:S(2)}) async-start(f32[8,48,128]{2,1,0:T(8,128)} %shard_map.94), calls=%async_computation | async-start | bytes 393216 | tf_op jit(solution)/shard_map/all_to_all | solution.py:211
  23.2 22.6 %copy-start.3 = (bf16[2048,128]{1,0:T(8,128)(2,1)S(1)}, bf16[2048,128]{1,0:T(8,128)(2,1)}, u32[]{:S(2)}) copy-start(bf16[2048,128]{1,0:T(8,128)(2,1)} %fact_ref.3) | copy-start | bytes 1572868

commit v2 on v1

v2 whole, which is shorter than its diff:
```python
import jax
import jax.numpy as jnp
from jax import lax
from jax.experimental import pallas as pl
from jax.experimental.pallas import tpu as pltpu
from jax.sharding import PartitionSpec as P

LANES = 128
OWNERS = 32
CHIPS = 16
PEERS = 8
DIM_ROWS = 32
FACT_ROWS = 16
FACTS_HERE = FACT_ROWS * LANES
SCORE_ROWS = DIM_ROWS + FACT_ROWS
BLOCK_ROWS = DIM_ROWS + 4
PIECE = 1024
OWNER_BIT = 7
LABEL_BIT = 12
VALID_BIT = 13

bf16 = jnp.bfloat16
f32 = jnp.float32


def split3(value):
    high = value.astype(bf16).astype(f32)
    rest = value - high
    middle = rest.astype(bf16).astype(f32)
    return high, middle, rest - middle


def stacked_row(row):
    shape = (8, row.shape[1])
    place = lax.broadcasted_iota(jnp.int32, shape, 0)
    high, middle, low = split3(row)
    return jnp.where(
        place == 0, high, jnp.where(place == 1, middle, jnp.where(place == 2, low, 0.0))
    ).astype(bf16)


def dot_nt(left, right):
    return lax.dot_general(
        left, right, (((1,), (1,)), ((), ())), preferred_element_type=f32
    )


def dot_nn(left, right):
    return jnp.dot(left, right, preferred_element_type=f32)


def hits(row, count):
    return lax.broadcasted_iota(jnp.int32, (count, row.shape[1]), 0) == row


def onehot(row, count):
    return jnp.where(hits(row, count), 1.0, 0.0).astype(bf16)


def scores_kernel(
    fact_hbm, dim_hbm, fact_weight_hbm, dim_weight_hbm, out_ref, fact, dim, weights, sems
):
    def copies(source, target, first):
        found = []
        for i in range(source.shape[0] // PIECE):
            cut = pl.ds(i * PIECE, PIECE)
            found.append(pltpu.make_async_copy(source.at[cut], target.at[cut], sems.at[first + i]))
        return found

    dim_pieces = copies(dim_hbm, dim, 2)
    fact_pieces = copies(fact_hbm, fact, 2 + len(dim_pieces))
    dim_weight = pltpu.make_async_copy(dim_weight_hbm, weights.at[pl.ds(0, 1)], sems.at[0])
    fact_weight = pltpu.make_async_copy(fact_weight_hbm, weights.at[pl.ds(1, 1)], sems.at[1])
    for copy in [dim_weight, fact_weight] + dim_pieces + fact_pieces:
        copy.start()
    row = 0
    for place, weight, table, pieces in (
        (0, dim_weight, dim, dim_pieces),
        (1, fact_weight, fact, fact_pieces),
    ):
        weight.wait()
        terms = stacked_row(weights[place : place + 1, :])
        for i, piece in enumerate(pieces):
            piece.wait()
            part = dot_nt(terms, table[i * PIECE : (i + 1) * PIECE, :])
            part = jnp.sum(part, 0, keepdims=True)
            for j in range(PIECE // LANES):
                out_ref[0, row : row + 1, :] = part[:, j * LANES : (j + 1) * LANES]
                row += 1
    for peer in range(1, PEERS):
        out_ref[peer] = out_ref[0]


def slots_kernel(core_ref, bucket_hbm, index_hbm, label_hbm, place_ref, meta_ref, given, sems):
    loads = [
        pltpu.make_async_copy(source, given.at[pl.ds(i, 1)], sems.at[i])
        for i, source in enumerate((bucket_hbm, index_hbm, label_hbm))
    ]
    for load in loads:
        load.start()
    width = 2 * LANES
    chunks = FACTS_HERE // width
    upto = jnp.where(
        lax.broadcasted_iota(jnp.int32, (width, width), 0)
        <= lax.broadcasted_iota(jnp.int32, (width, width), 1),
        1.0,
        0.0,
    ).astype(bf16)
    for load in loads:
        load.wait()
    bucket = given[0:1, :]
    owner = (bucket >> 1) + ((bucket & 1) ^ core_ref[0]) * CHIPS
    label = given[2:3, :]
    owner_hits = onehot(owner, OWNERS)
    stack = jnp.concatenate(
        [owner_hits[:, c * width : (c + 1) * width] for c in range(chunks)], 0
    )
    prefix = dot_nn(stack, upto)
    before = jnp.zeros((OWNERS, 1), f32)
    ranks = []
    for c in range(chunks):
        here = prefix[c * OWNERS : (c + 1) * OWNERS]
        mine = hits(owner[:, c * width : (c + 1) * width], OWNERS)
        ranks.append(jnp.sum(jnp.where(mine, here + before, 0.0), 0, keepdims=True))
        before = before + here[:, width - 1 : width]
    rank = jnp.concatenate(ranks, 1).astype(jnp.int32) - 1
    place_ref[...] = rank + (owner << OWNER_BIT) + (label << LABEL_BIT)
    index = given[1:2, :]
    low = (index & (LANES - 1)).astype(f32)
    high = ((index >> 7) + (label << (LABEL_BIT - 7)) + (1 << (VALID_BIT - 7))).astype(f32)
    mine = hits(owner, OWNERS)
    fields = jnp.concatenate([jnp.where(mine, low, 0.0), jnp.where(mine, high, 0.0)], 0)
    packed = dot_nt(fields.astype(bf16), onehot(rank, LANES))
    meta_ref[...] = packed[:OWNERS] + packed[OWNERS:] * LANES


def places(place_ref):
    place = place_ref[...]
    return place & (LANES - 1), (place >> OWNER_BIT) & (OWNERS - 1), place >> LABEL_BIT


def pack_kernel(recv_ref, place_ref, meta_ref, out_ref, dims_ref, facts_ref, left_ref):
    total = recv_ref[0]
    for peer in range(1, PEERS):
        total = total + recv_ref[peer]
    dims_ref[...] = total[:DIM_ROWS]
    rank, owner, _ = places(place_ref)
    for i in range(FACT_ROWS):
        cut = slice(i * LANES, (i + 1) * LANES)
        mine = hits(owner[:, cut], OWNERS)
        for part, value in enumerate(split3(total[DIM_ROWS + i : DIM_ROWS + i + 1])):
            left_ref[part * OWNERS : (part + 1) * OWNERS, cut] = jnp.where(mine, value, 0.0).astype(bf16)
    packed = dot_nt(left_ref[...], onehot(rank, LANES))
    packed = packed[:OWNERS] + packed[OWNERS : 2 * OWNERS] + packed[2 * OWNERS :]
    facts_ref[...] = packed
    for chip in range(CHIPS):
        out_ref[chip, :DIM_ROWS, :] = total[:DIM_ROWS]
        for other in range(2):
            row, slot = DIM_ROWS + other, other * CHIPS + chip
            out_ref[chip, row : row + 1, :] = packed[slot : slot + 1]
            out_ref[chip, row + 2 : row + 3, :] = meta_ref[slot : slot + 1, :]


def stacked(value):
    return jnp.concatenate(split3(value), 0).astype(bf16)


def found(parts, row):
    count = parts.shape[0] // 3
    value = parts[:count] + parts[count : 2 * count] + parts[2 * count :]
    return jnp.sum(jnp.where(hits(row, count), value, 0.0), 0, keepdims=True)


def sigmoid(value):
    return 1.0 / (1.0 + jnp.exp(-value))


def half(other, recv_ref, dims_ref, facts_ref, meta_ref, place_ref, scratch):
    home_ref, own_ref, code_ref, low_ref, left_ref = scratch
    slots = slice(other * CHIPS, (other + 1) * CHIPS)
    meta = meta_ref[slots, :].astype(jnp.int32)
    dims = stacked(dims_ref[...])
    for chip in range(CHIPS):
        code = meta[chip : chip + 1]
        parts = dot_nn(stacked(recv_ref[chip, :DIM_ROWS, :]), onehot(code & (LANES - 1), LANES))
        home_ref[chip : chip + 1, :] = found(parts, (code >> 7) & (DIM_ROWS - 1))
        row = DIM_ROWS + other
        cut = slice(chip * LANES, (chip + 1) * LANES)
        code = recv_ref[chip, row + 2 : row + 3, :].astype(jnp.int32)
        code_ref[chip : chip + 1, :] = code
        column = onehot(code & (LANES - 1), LANES)
        low_ref[:, cut] = column
        own_ref[chip : chip + 1, :] = recv_ref[chip, row : row + 1, :] + found(
            dot_nn(dims, column), (code >> 7) & (DIM_ROWS - 1)
        )
    rank, owner, _ = places(place_ref)
    prob = sigmoid(home_ref[...] + facts_ref[slots, :])
    prob = found(dot_nn(stacked(prob), onehot(rank, LANES)), owner - other * CHIPS)
    code = code_ref[...]
    residual = (sigmoid(own_ref[...]) - ((code >> LABEL_BIT) & 1).astype(f32)) * (
        code >> VALID_BIT
    ).astype(f32)
    terms = split3(residual)
    for chip in range(CHIPS):
        cut = slice(chip * LANES, (chip + 1) * LANES)
        mine = hits((code[chip : chip + 1] >> 7) & (DIM_ROWS - 1), DIM_ROWS)
        for part, value in enumerate(terms):
            left_ref[part * DIM_ROWS : (part + 1) * DIM_ROWS, cut] = jnp.where(
                mine, value[chip : chip + 1], 0.0
            ).astype(bf16)
    sums = dot_nt(left_ref[...], low_ref[...])
    return prob, sums[:DIM_ROWS] + sums[DIM_ROWS : 2 * DIM_ROWS] + sums[2 * DIM_ROWS :]


def same_core_kernel(
    recv_ref, dims_ref, facts_ref, meta_ref, place_ref, prob_ref, sums_ref, *scratch
):
    prob_ref[...], sums_ref[...] = half(
        0, recv_ref, dims_ref, facts_ref, meta_ref, place_ref, scratch
    )


def grads_kernel(
    recv_ref,
    dims_ref,
    facts_ref,
    meta_ref,
    place_ref,
    prob_half_ref,
    sums_half_ref,
    fact_ref,
    dim_ref,
    out_ref,
    prob_ref,
    *scratch,
):
    prob, sums = half(1, recv_ref, dims_ref, facts_ref, meta_ref, place_ref, scratch)
    prob = prob + prob_half_ref[...]
    sums = sums + sums_half_ref[...]
    prob_ref[...] = prob
    residual = prob - places(place_ref)[2].astype(f32)
    grad_fact = jnp.sum(dot_nn(stacked_row(residual), fact_ref[...]), 0, keepdims=True)
    rows = jnp.concatenate([stacked_row(sums[i : i + 1]) for i in range(DIM_ROWS)], 1)
    grad_dim = jnp.sum(dot_nn(rows, dim_ref[...]), 0, keepdims=True)
    for owner in range(OWNERS):
        out_ref[owner, 0:1, :] = grad_fact
        out_ref[owner, 1:2, :] = grad_dim


def update_kernel(recv_ref, fact_weight_ref, dim_weight_ref, fact_out_ref, dim_out_ref):
    total = recv_ref[0]
    for peer in range(1, OWNERS):
        total = total + recv_ref[peer]
    scale = 0.5 / (OWNERS * FACTS_HERE) ** 0.5
    fact_out_ref[...] = fact_weight_ref[...] - scale * total[0:1]
    dim_out_ref[...] = dim_weight_ref[...] - scale * total[1:2]


HALF_SCRATCH = [
    pltpu.VMEM((CHIPS, LANES), f32),
    pltpu.VMEM((CHIPS, LANES), f32),
    pltpu.VMEM((CHIPS, LANES), jnp.int32),
    pltpu.VMEM((LANES, CHIPS * LANES), bf16),
    pltpu.VMEM((3 * DIM_ROWS, CHIPS * LANES), bf16),
]


def call(kernel, outs, scratch=(), in_specs=None, flops=None, vmem=32 << 20):
    extra = {} if in_specs is None else {"in_specs": in_specs}
    if flops is not None:
        extra["cost_estimate"] = pl.CostEstimate(
            flops=flops, bytes_accessed=1 << 20, transcendentals=0
        )
    return pl.pallas_call(
        kernel,
        out_shape=[jax.ShapeDtypeStruct(shape, dtype) for shape, dtype in outs],
        scratch_shapes=list(scratch),
        compiler_params=pltpu.CompilerParams(vmem_limit_bytes=vmem),
        **extra,
    )


def exchange(value, axis, groups=None):
    return lax.all_to_all(
        value, axis, split_axis=0, concat_axis=0, tiled=True, axis_index_groups=groups
    )


def shards(fact_table, dim_table, fact_weight, dim_weight, bucket, row_index, labels):
    bucket = bucket.reshape(1, FACTS_HERE)
    row_index = row_index.reshape(1, FACTS_HERE)
    labels = labels.reshape(1, FACTS_HERE)
    fact_weight = fact_weight.reshape(1, LANES)
    dim_weight = dim_weight.reshape(1, LANES)
    core = (lax.axis_index("rows") & 1).reshape(1)
    in_hbm = pl.BlockSpec(memory_space=pltpu.HBM)

    (partial,) = call(
        scores_kernel,
        [((PEERS, SCORE_ROWS, LANES), f32)],
        [
            pltpu.VMEM(fact_table.shape, bf16),
            pltpu.VMEM(dim_table.shape, bf16),
            pltpu.VMEM((2, LANES), f32),
            pltpu.SemaphoreType.DMA((2 + (len(fact_table) + len(dim_table)) // PIECE,)),
        ],
        [in_hbm] * 4,
        vmem=(63 << 20) + (1 << 19),
    )(fact_table, dim_table, fact_weight, dim_weight)
    place, meta = call(
        slots_kernel,
        [((1, FACTS_HERE), jnp.int32), ((OWNERS, LANES), f32)],
        [pltpu.VMEM((3, FACTS_HERE), jnp.int32), pltpu.SemaphoreType.DMA((3,))],
        [pl.BlockSpec(memory_space=pltpu.SMEM)] + [in_hbm] * 3,
    )(core, bucket, row_index, labels)
    partial = exchange(partial, "feat")
    blocks, dims, facts = call(
        pack_kernel,
        [((CHIPS, BLOCK_ROWS, LANES), f32), ((DIM_ROWS, LANES), f32), ((OWNERS, LANES), f32)],
        [pltpu.VMEM((3 * OWNERS, FACTS_HERE), bf16)],
    )(partial, place, meta)
    blocks = exchange(
        blocks, "rows", [[2 * chip + core for chip in range(CHIPS)] for core in range(2)]
    )
    other_blocks = lax.ppermute(blocks, "rows", [(i, i ^ 1) for i in range(OWNERS)])
    prob_half, sums_half = call(
        same_core_kernel,
        [((1, FACTS_HERE), f32), ((DIM_ROWS, LANES), f32)],
        HALF_SCRATCH,
        flops=1 << 31,
    )(blocks, dims, facts, meta, place)
    grads, prob = call(
        grads_kernel,
        [((OWNERS, 2, LANES), f32), ((1, FACTS_HERE), f32)],
        HALF_SCRATCH,
    )(other_blocks, dims, facts, meta, place, prob_half, sums_half, fact_table, dim_table)
    grads = exchange(grads, "rows")
    new_fact, new_dim = call(update_kernel, [((1, LANES), f32), ((1, LANES), f32)])(
        grads, fact_weight, dim_weight
    )
    return new_fact.reshape(-1), new_dim.reshape(-1), prob.reshape(-1)


def solution(mesh):
    return jax.shard_map(
        shards,
        mesh=mesh,
        in_specs=(
            P("rows", "feat"),
            P("rows", "feat"),
            P("feat"),
            P("feat"),
            P("rows", None),
            P("rows"),
            P("rows"),
        ),
        out_specs=(P("feat"), P("feat"), P("rows")),
        check_vma=False,
    )
```

time: 60.3 us -> 55.3 us (0.917)
  blocking collectives: 33.3 us -> 25.5 us
  starting transfers between devices: 9.15 us -> 13 us
  local copies, waits for them, and re-layouts: 2.94 us -> 0.81 us
  Pallas kernels: 5.56 us -> 7.32 us
    all_to_all x2, blocking collectives: 33.3 us -> 25.5 us  [exchange(): lax.all_to_all(value, axis, split_axis=0, concat_axis=0, tiled=True, axis...]
    ppermute x0 -> x1, starting transfers between devices: none -> 3.96 us  [shards(): lax.ppermute(blocks, 'rows', [(i, i ^ 1) for i in range(OWNERS)])]
    unnamed x18 -> x14, local copies, waits for them, and re-layouts: 2.94 us -> 0.81 us
    pallas_call x4 -> x5, Pallas kernels: 5.01 us -> 6.77 us  [the longest x1 2.9 us: shards(): call(scores_kernel, [((PEERS, SCORE_ROWS, LANES), f32)], [pltpu.VMEM(fact...]
    all_to_all x1, waiting for transfers between devices: 8.18 us -> 7.43 us  [exchange(): lax.all_to_all(value, axis, split_axis=0, concat_axis=0, tiled=True, axis...]
  transfers between devices with their start and end apart: 1 -> 2, of which waited for: 1 -> 2; matrix products, arithmetic and copies ran while one was open for 0% -> 0% of each run, Pallas kernels for 1% -> 3%
where the time goes in v2:
time: 55.3 us; the launch traced here: 55 us
  blocking collectives  25.5 us (46%)
  starting transfers between devices  13 us (24%)
  waiting for transfers between devices  7.64 us (14%)
  Pallas kernels  7.32 us (13%)
  local copies, waits for them, and re-layouts  0.81 us (1%)
  between operations  0.68 us (1%)
    all_to_all x2, blocking collectives, exchange(): lax.all_to_all(value, axis, split_axis=0, concat_axis=0, tiled=True, axis...  25.5 us
    all_to_all x1, starting transfers between devices, exchange(): lax.all_to_all(value, axis, split_axis=0, concat_axis=0, tiled=True, axis...  9.03 us
    all_to_all x1, waiting for transfers between devices, exchange(): lax.all_to_all(value, axis, split_axis=0, concat_axis=0, tiled=True, axis...  7.43 us
    ppermute x1, starting transfers between devices, shards(): lax.ppermute(blocks, 'rows', [(i, i ^ 1) for i in range(OWNERS)])  3.96 us
    pallas_call x1, Pallas kernels, shards(): call(scores_kernel, [((PEERS, SCORE_ROWS, LANES), f32)], [pltpu.VMEM(fact...  2.9 us
    pallas_call x1, Pallas kernels, shards(): call(grads_kernel, [((OWNERS, 2, LANES), f32), ((1, FACTS_HERE), f32)], H...  1.79 us
  transfers between devices with their start and end apart: 2, of which 2 were waited for; matrix products, arithmetic and copies ran while one was open for 0% of the time, Pallas kernels for 3%

profile of v2, /device:TPU:1, one launch (start us, length us, event | category | flops | bytes accessed | tf_op | source)
XLA Modules:
  0.0 55.0 jit_solution(7216662565739038798)
XLA Ops:
  0.6 2.9 %shard_map.94 = f32[8,48,128]{2,1,0:T(8,128)} custom-call(bf16[2048,128]{1,0:T(8,128)(2,1)} %fact_ref.1, bf16[4096,128]{1,0:T(8,128)(2,1)} %dim_ref.1, f32[1,128]{1,0:T(1,128)} %bitcast.12, f32[1,128]{1,0:T(1,128)} %bitcast.14), custom_call_target="tpu_custom_call" | custom-call | tf_op jit(solution)/shard_map/pallas_call | solution.py:298
  3.5 0.0 copy-start.4
  3.5 9.0 %all-to-all-start = ((f32[8,48,128]{2,1,0:T(8,128)}), f32[8,48,128]{2,1,0:T(8,128)S(1)}, u32[]{:S(2)}, u32[]{:S(2)}) async-start(f32[8,48,128]{2,1,0:T(8,128)} %shard_map.94), calls=%async_computation | async-start | bytes 393216 | tf_op jit(solution)/shard_map/all_to_all | solution.py:284
  12.6 0.0 copy-start.3
  12.6 0.0 copy-start.2
  12.6 0.0 copy-done.4
  12.6 0.7 %copy-done.3 = s32[2048]{0:T(1024)S(1)} copy-done((s32[2048]{0:T(1024)S(1)}, s32[2048]{0:T(1024)}, u32[]{:S(2)}) %copy-start.3) | copy-done | bytes 8216
  13.3 0.0 copy-done.2
  13.3 0.7 %shard_map.95 = (s32[1,2048]{1,0:T(1,128)S(1)}, f32[32,128]{1,0:T(8,128)S(1)}) custom-call(s32[1]{0:T(128)} %bitcast.2.core_ref, s32[1,2048]{1,0:T(1,128)S(1)} %bitcast.9, s32[1,2048]{1,0:T(1,128)S(1)} %bitcast.10, s32[1,2048]{1,0:T(1,128)S(1)} %bitcast.11), custom_call_target="tpu_custom_call" | custom-call | tf_op jit(solution)/shard_map/pallas_call | solution.py:310
  14.0 7.4 %all-to-all-done.recv_ref = f32[8,48,128]{2,1,0:T(8,128)S(1)} async-done(((f32[8,48,128]{2,1,0:T(8,128)}), f32[8,48,128]{2,1,0:T(8,128)S(1)}, u32[]{:S(2)}, u32[]{:S(2)}) %all-to-all-start) | async-done | bytes 196640 | tf_op jit(solution)/shard_map/all_to_all | solution.py:284
  21.4 0.4 shard_map.96
  21.8 14.3 %all_to_all.15.recv_ref = f32[16,36,128]{2,1,0:T(8,128)S(1)} all-to-all(f32[16,36,128]{2,1,0:T(8,128)S(1)} %get-tuple-element.16), channel_id=1, replica_groups={{0,16,32,48,64,80,96,112,128,144,160,176,192,208,224,240},{8,24,40,56,7..., dimensions={0} | all-to-all | bytes 589824 | tf_op jit(solution)/shard_map/all_to_all | solution.py:284
  36.1 4.0 %collective-permute-start = (f32[16,36,128]{2,1,0:T(8,128)S(1)}, f32[16,36,128]{2,1,0:T(8,128)S(1)}, u32[]{:S(2)}, u32[]{:S(2)}) collective-permute-start(f32[16,36,128]{2,1,0:T(8,128)S(1)} %all_to_all.15.recv_ref), channel_id=1, source_target_pairs={{0,8},{8,0},{16,24},{24,16},{32,40},{40,32},{48,56},{56,48},{64,72... | collective-permute-start | bytes 884744 | tf_op jit(solution)/shard_map/ppermute | solution.py:325
  40.1 0.0 copy-start
  40.1 0.0 copy-start.1
  40.1 1.0 %shard_map.97 = (f32[1,2048]{1,0:T(1,128)S(1)}, f32[32,128]{1,0:T(8,128)S(1)}) custom-call(f32[16,36,128]{2,1,0:T(8,128)S(1)} %all_to_all.15.recv_ref, f32[32,128]{1,0:T(8,128)S(1)} %get-tuple-element.17.dims_ref, f32[32,128]{1,0:T(8,128)S(1)} %get-tuple-element.18.facts_ref, f32[32,128]{1,0:T(8,128)S(1)} %get-tuple-element.15.meta_ref, ...), custom_call_target="tpu_custom_call" | custom-call | flops 2147483648 | bytes 1048576 | tf_op jit(solution)/shard_map/pallas_call | solution.py:326
  41.1 0.2 collective-permute-done.recv_ref
  41.3 0.0 copy-done
  41.3 0.1 copy-done.1
  41.4 1.8 %shard_map.98 = (f32[32,2,128]{2,1,0:T(2,128)S(1)}, f32[1,2048]{1,0:T(1,128)}) custom-call(f32[16,36,128]{2,1,0:T(8,128)S(1)} %collective-permute-done.recv_ref, f32[32,128]{1,0:T(8,128)S(1)} %get-tuple-element.17.dims_ref, f32[32,128]{1,0:T(8,128)S(1)} %get-tuple-element.18.facts_ref, f32[32,128]{1,0:T(8,128)S(1)} %get-tuple-element.15.meta_ref, ...), custom_call_target="tpu_custom_call" | custom-call | tf_op jit(solution)/shard_map/pallas_call | solution.py:332
  43.2 0.0 copy-start.5
  43.2 0.0 copy-start.6
  43.2 11.2 %all_to_all.16.recv_ref = f32[32,2,128]{2,1,0:T(2,128)S(1)} all-to-all(f32[32,2,128]{2,1,0:T(2,128)S(1)} %get-tuple-element.21), channel_id=1, replica_groups=mesh['rows'=32,'feat'=8] {'rows'}, dimensions={0} | all-to-all | bytes 65536 | tf_op jit(solution)/shard_map/all_to_all | solution.py:284
  54.4 0.0 copy-done.5
  54.4 0.0 copy-done.6
  54.4 0.6 %shard_map.99 = (f32[1,128]{1,0:T(1,128)}, f32[1,128]{1,0:T(1,128)}) custom-call(f32[32,2,128]{2,1,0:T(2,128)S(1)} %all_to_all.16.recv_ref, f32[1,128]{1,0:T(1,128)S(1)} %bitcast.13, f32[1,128]{1,0:T(1,128)S(1)} %bitcast.15), custom_call_target="tpu_custom_call" | custom-call | tf_op jit(solution)/shard_map/pallas_call | solution.py:338
Async XLA Ops:
  3.5 9.1 %copy-start.4 = (s32[2048]{0:T(1024)S(1)}, s32[2048]{0:T(1024)}, u32[]{:S(2)}) copy-start(s32[2048]{0:T(1024)} %param.13) | copy-start | bytes 24580
  3.5 17.8 %all-to-all-start = ((f32[8,48,128]{2,1,0:T(8,128)}), f32[8,48,128]{2,1,0:T(8,128)S(1)}, u32[]{:S(2)}, u32[]{:S(2)}) async-start(f32[8,48,128]{2,1,0:T(8,128)} %shard_map.94), calls=%async_computation | async-start | bytes 393216 | tf_op jit(solution)/shard_map/all_to_all | solution.py:284
  12.6 0.7 %copy-start.3 = (s32[2048]{0:T(1024)S(1)}, s32[2048]{0:T(1024)}, u32[]{:S(2)}) copy-start(s32[2048]{0:T(1024)} %param.12) | copy-start | bytes 24580
  12.6 0.7 %copy-start.2 = (s32[2048,1]{0,1:T(1,128)S(1)}, s32[2048,1]{0,1:T(1,128)}, u32[]{:S(2)}) copy-start(s32[2048,1]{0,1:T(1,128)} %param.11) | copy-start | bytes 24580
  36.1 5.2 %collective-permute-start = (f32[16,36,128]{2,1,0:T(8,128)S(1)}, f32[16,36,128]{2,1,0:T(8,128)S(1)}, u32[]{:S(2)}, u32[]{:S(2)}) collective-permute-start(f32[16,36,128]{2,1,0:T(8,128)S(1)} %all_to_all.15.recv_ref), channel_id=1, source_target_pairs={{0,8},{8,0},{16,24},{24,16},{32,40},{40,32},{48,56},{56,48},{64,72... | collective-permute-start | bytes 884744 | tf_op jit(solution)/shard_map/ppermute | solution.py:325
  40.1 1.3 %copy-start = (bf16[4096,128]{1,0:T(8,128)(2,1)S(1)}, bf16[4096,128]{1,0:T(8,128)(2,1)}, u32[]{:S(2)}) copy-start(bf16[4096,128]{1,0:T(8,128)(2,1)} %dim_ref.1) | copy-start | bytes 3145732
  40.1 1.4 %copy-start.1 = (bf16[2048,128]{1,0:T(8,128)(2,1)S(1)}, bf16[2048,128]{1,0:T(8,128)(2,1)}, u32[]{:S(2)}) copy-start(bf16[2048,128]{1,0:T(8,128)(2,1)} %fact_ref.1) | copy-start | bytes 1572868
  43.2 11.2 %copy-start.5 = (f32[128]{0:T(128)S(1)}, f32[128]{0:T(128)}, u32[]{:S(2)}) copy-start(f32[128]{0:T(128)} %param.9) | copy-start | bytes 1540
  43.2 11.2 %copy-start.6 = (f32[128]{0:T(128)S(1)}, f32[128]{0:T(128)}, u32[]{:S(2)}) copy-start(f32[128]{0:T(128)} %param.10) | copy-start | bytes 1540

commit v3 on v2

--- a/solution.py
+++ b/solution.py
@@ -14,8 +14,7 @@
 FACTS_HERE = FACT_ROWS * LANES
 SCORE_ROWS = DIM_ROWS + FACT_ROWS
 BLOCK_ROWS = DIM_ROWS + 4
-PIECE = 1024
-OWNER_BIT = 7
+PIECE = 2048
 LABEL_BIT = 12
 VALID_BIT = 13
 
@@ -71,27 +70,36 @@
     fact_pieces = copies(fact_hbm, fact, 2 + len(dim_pieces))
     dim_weight = pltpu.make_async_copy(dim_weight_hbm, weights.at[pl.ds(0, 1)], sems.at[0])
     fact_weight = pltpu.make_async_copy(fact_weight_hbm, weights.at[pl.ds(1, 1)], sems.at[1])
-    for copy in [dim_weight, fact_weight] + dim_pieces + fact_pieces:
+    for copy in [dim_weight, fact_weight] + fact_pieces + dim_pieces:
         copy.start()
-    row = 0
-    for place, weight, table, pieces in (
-        (0, dim_weight, dim, dim_pieces),
-        (1, fact_weight, fact, fact_pieces),
+    for row, place, weight, table, pieces in (
+        (DIM_ROWS, 1, fact_weight, fact, fact_pieces),
+        (0, 0, dim_weight, dim, dim_pieces),
     ):
         weight.wait()
-        terms = stacked_row(weights[place : place + 1, :])
-        for i, piece in enumerate(pieces):
+        for piece in pieces:
             piece.wait()
-            part = dot_nt(terms, table[i * PIECE : (i + 1) * PIECE, :])
-            part = jnp.sum(part, 0, keepdims=True)
-            for j in range(PIECE // LANES):
-                out_ref[0, row : row + 1, :] = part[:, j * LANES : (j + 1) * LANES]
-                row += 1
+        part = dot_nt(stacked_row(weights[place : place + 1, :]), table[...])
+        part = jnp.sum(part, 0, keepdims=True)
+        for i in range(table.shape[0] // LANES):
+            out_ref[0, row : row + 1, :] = part[:, i * LANES : (i + 1) * LANES]
+            row += 1
     for peer in range(1, PEERS):
         out_ref[peer] = out_ref[0]
 
 
-def slots_kernel(core_ref, bucket_hbm, index_hbm, label_hbm, place_ref, meta_ref, given, sems):
+def slots_kernel(
+    core_ref,
+    bucket_hbm,
+    index_hbm,
+    label_hbm,
+    place_ref,
+    meta_ref,
+    rank_hits_ref,
+    row_hits_ref,
+    given,
+    sems,
+):
     loads = [
         pltpu.make_async_copy(source, given.at[pl.ds(i, 1)], sems.at[i])
         for i, source in enumerate((bucket_hbm, index_hbm, label_hbm))
@@ -124,33 +132,41 @@
         ranks.append(jnp.sum(jnp.where(mine, here + before, 0.0), 0, keepdims=True))
         before = before + here[:, width - 1 : width]
     rank = jnp.concatenate(ranks, 1).astype(jnp.int32) - 1
-    place_ref[...] = rank + (owner << OWNER_BIT) + (label << LABEL_BIT)
+    place_ref[...] = owner + (label << LABEL_BIT)
     index = given[1:2, :]
     low = (index & (LANES - 1)).astype(f32)
     high = ((index >> 7) + (label << (LABEL_BIT - 7)) + (1 << (VALID_BIT - 7))).astype(f32)
     mine = hits(owner, OWNERS)
     fields = jnp.concatenate([jnp.where(mine, low, 0.0), jnp.where(mine, high, 0.0)], 0)
-    packed = dot_nt(fields.astype(bf16), onehot(rank, LANES))
+    rank_hits = onehot(rank, LANES)
+    rank_hits_ref[...] = rank_hits
+    packed = dot_nt(fields.astype(bf16), rank_hits)
     meta_ref[...] = packed[:OWNERS] + packed[OWNERS:] * LANES
+    low = packed[:OWNERS].astype(jnp.int32)
+    for owner in range(OWNERS):
+        cut = slice(owner * LANES, (owner + 1) * LANES)
+        row_hits_ref[:, cut] = onehot(low[owner : owner + 1], LANES)
 
 
 def places(place_ref):
     place = place_ref[...]
-    return place & (LANES - 1), (place >> OWNER_BIT) & (OWNERS - 1), place >> LABEL_BIT
-
-
-def pack_kernel(recv_ref, place_ref, meta_ref, out_ref, dims_ref, facts_ref, left_ref):
+    return place & (OWNERS - 1), place >> LABEL_BIT
+
+
+def pack_kernel(
+    recv_ref, place_ref, meta_ref, rank_hits_ref, out_ref, dims_ref, facts_ref, left_ref
+):
     total = recv_ref[0]
     for peer in range(1, PEERS):
         total = total + recv_ref[peer]
     dims_ref[...] = total[:DIM_ROWS]
-    rank, owner, _ = places(place_ref)
+    owner, _ = places(place_ref)
     for i in range(FACT_ROWS):
         cut = slice(i * LANES, (i + 1) * LANES)
         mine = hits(owner[:, cut], OWNERS)
         for part, value in enumerate(split3(total[DIM_ROWS + i : DIM_ROWS + i + 1])):
             left_ref[part * OWNERS : (part + 1) * OWNERS, cut] = jnp.where(mine, value, 0.0).astype(bf16)
-    packed = dot_nt(left_ref[...], onehot(rank, LANES))
+    packed = dot_nt(left_ref[...], rank_hits_ref[...])
     packed = packed[:OWNERS] + packed[OWNERS : 2 * OWNERS] + packed[2 * OWNERS :]
     facts_ref[...] = packed
     for chip in range(CHIPS):
@@ -161,46 +177,56 @@
             out_ref[chip, row + 2 : row + 3, :] = meta_ref[slot : slot + 1, :]
 
 
-def stacked(value):
-    return jnp.concatenate(split3(value), 0).astype(bf16)
-
-
-def found(parts, row):
-    count = parts.shape[0] // 3
-    value = parts[:count] + parts[count : 2 * count] + parts[2 * count :]
-    return jnp.sum(jnp.where(hits(row, count), value, 0.0), 0, keepdims=True)
+def stacked(value, count=3):
+    return jnp.concatenate(split3(value)[:count], 0).astype(bf16)
+
+
+def summed(parts, count):
+    total = parts[:count]
+    for start in range(count, parts.shape[0], count):
+        total = total + parts[start : start + count]
+    return total
+
+
+def taken(value, row):
+    return jnp.sum(jnp.where(hits(row, value.shape[0]), value, 0.0), 0, keepdims=True)
 
 
 def sigmoid(value):
     return 1.0 / (1.0 + jnp.exp(-value))
 
 
-def half(other, recv_ref, dims_ref, facts_ref, meta_ref, place_ref, scratch):
+def half(
+    other, recv_ref, dims_ref, facts_ref, meta_ref, place_ref, rank_hits_ref, row_hits_ref, scratch
+):
     home_ref, own_ref, code_ref, low_ref, left_ref = scratch
     slots = slice(other * CHIPS, (other + 1) * CHIPS)
     meta = meta_ref[slots, :].astype(jnp.int32)
     dims = stacked(dims_ref[...])
     for chip in range(CHIPS):
-        code = meta[chip : chip + 1]
-        parts = dot_nn(stacked(recv_ref[chip, :DIM_ROWS, :]), onehot(code & (LANES - 1), LANES))
-        home_ref[chip : chip + 1, :] = found(parts, (code >> 7) & (DIM_ROWS - 1))
+        cut = slice((other * CHIPS + chip) * LANES, (other * CHIPS + chip + 1) * LANES)
+        parts = dot_nn(stacked(recv_ref[chip, :DIM_ROWS, :]), row_hits_ref[:, cut])
+        home_ref[chip : chip + 1, :] = taken(
+            summed(parts, DIM_ROWS), (meta[chip : chip + 1] >> 7) & (DIM_ROWS - 1)
+        )
         row = DIM_ROWS + other
         cut = slice(chip * LANES, (chip + 1) * LANES)
         code = recv_ref[chip, row + 2 : row + 3, :].astype(jnp.int32)
         code_ref[chip : chip + 1, :] = code
         column = onehot(code & (LANES - 1), LANES)
         low_ref[:, cut] = column
-        own_ref[chip : chip + 1, :] = recv_ref[chip, row : row + 1, :] + found(
-            dot_nn(dims, column), (code >> 7) & (DIM_ROWS - 1)
+        own_ref[chip : chip + 1, :] = recv_ref[chip, row : row + 1, :] + taken(
+            summed(dot_nn(dims, column), DIM_ROWS), (code >> 7) & (DIM_ROWS - 1)
         )
-    rank, owner, _ = places(place_ref)
-    prob = sigmoid(home_ref[...] + facts_ref[slots, :])
-    prob = found(dot_nn(stacked(prob), onehot(rank, LANES)), owner - other * CHIPS)
+    prob = stacked(sigmoid(home_ref[...] + facts_ref[slots, :]), 2)
+    prob = taken(
+        summed(dot_nn(prob, rank_hits_ref[...]), CHIPS), places(place_ref)[0] - other * CHIPS
+    )
     code = code_ref[...]
     residual = (sigmoid(own_ref[...]) - ((code >> LABEL_BIT) & 1).astype(f32)) * (
         code >> VALID_BIT
     ).astype(f32)
-    terms = split3(residual)
+    terms = split3(residual)[:2]
     for chip in range(CHIPS):
         cut = slice(chip * LANES, (chip + 1) * LANES)
         mine = hits((code[chip : chip + 1] >> 7) & (DIM_ROWS - 1), DIM_ROWS)
@@ -208,15 +234,23 @@
             left_ref[part * DIM_ROWS : (part + 1) * DIM_ROWS, cut] = jnp.where(
                 mine, value[chip : chip + 1], 0.0
             ).astype(bf16)
-    sums = dot_nt(left_ref[...], low_ref[...])
-    return prob, sums[:DIM_ROWS] + sums[DIM_ROWS : 2 * DIM_ROWS] + sums[2 * DIM_ROWS :]
+    return prob, summed(dot_nt(left_ref[...], low_ref[...]), DIM_ROWS)
 
 
 def same_core_kernel(
-    recv_ref, dims_ref, facts_ref, meta_ref, place_ref, prob_ref, sums_ref, *scratch
+    recv_ref,
+    dims_ref,
+    facts_ref,
+    meta_ref,
+    place_ref,
+    rank_hits_ref,
+    row_hits_ref,
+    prob_ref,
+    sums_ref,
+    *scratch,
 ):
     prob_ref[...], sums_ref[...] = half(
-        0, recv_ref, dims_ref, facts_ref, meta_ref, place_ref, scratch
+        0, recv_ref, dims_ref, facts_ref, meta_ref, place_ref, rank_hits_ref, row_hits_ref, scratch
     )
 
 
@@ -226,6 +260,8 @@
     facts_ref,
     meta_ref,
     place_ref,
+    rank_hits_ref,
+    row_hits_ref,
     prob_half_ref,
     sums_half_ref,
     fact_ref,
@@ -234,14 +270,21 @@
     prob_ref,
     *scratch,
 ):
-    prob, sums = half(1, recv_ref, dims_ref, facts_ref, meta_ref, place_ref, scratch)
+    prob, sums = half(
+        1, recv_ref, dims_ref, facts_ref, meta_ref, place_ref, rank_hits_ref, row_hits_ref, scratch
+    )
     prob = prob + prob_half_ref[...]
     sums = sums + sums_half_ref[...]
     prob_ref[...] = prob
-    residual = prob - places(place_ref)[2].astype(f32)
+    residual = prob - places(place_ref)[1].astype(f32)
     grad_fact = jnp.sum(dot_nn(stacked_row(residual), fact_ref[...]), 0, keepdims=True)
     rows = jnp.concatenate([stacked_row(sums[i : i + 1]) for i in range(DIM_ROWS)], 1)
-    grad_dim = jnp.sum(dot_nn(rows, dim_ref[...]), 0, keepdims=True)
+    side = DIM_ROWS // 2 * LANES
+    both = dot_nn(
+        jnp.concatenate([rows[:, :side], rows[:, side:]], 0),
+        jnp.concatenate([dim_ref[:side, :], dim_ref[side:, :]], 1),
+    )
+    grad_dim = jnp.sum(both[:8, :LANES] + both[8:, LANES:], 0, keepdims=True)
     for owner in range(OWNERS):
         out_ref[owner, 0:1, :] = grad_fact
         out_ref[owner, 1:2, :] = grad_dim
@@ -261,7 +304,7 @@
     pltpu.VMEM((CHIPS, LANES), f32),
     pltpu.VMEM((CHIPS, LANES), jnp.int32),
     pltpu.VMEM((LANES, CHIPS * LANES), bf16),
-    pltpu.VMEM((3 * DIM_ROWS, CHIPS * LANES), bf16),
+    pltpu.VMEM((2 * DIM_ROWS, CHIPS * LANES), bf16),
 ]
 
 
@@ -273,6 +316,7 @@
         )
     return pl.pallas_call(
         kernel,
+        name=kernel.__name__,
         out_shape=[jax.ShapeDtypeStruct(shape, dtype) for shape, dtype in outs],
         scratch_shapes=list(scratch),
         compiler_params=pltpu.CompilerParams(vmem_limit_bytes=vmem),
@@ -305,11 +349,16 @@
             pltpu.SemaphoreType.DMA((2 + (len(fact_table) + len(dim_table)) // PIECE,)),
         ],
         [in_hbm] * 4,
-        vmem=(63 << 20) + (1 << 19),
+        vmem=(53 << 20) + (1 << 19),
     )(fact_table, dim_table, fact_weight, dim_weight)
-    place, meta = call(
+    place, meta, rank_hits, row_hits = call(
         slots_kernel,
-        [((1, FACTS_HERE), jnp.int32), ((OWNERS, LANES), f32)],
+        [
+            ((1, FACTS_HERE), jnp.int32),
+            ((OWNERS, LANES), f32),
+            ((LANES, FACTS_HERE), bf16),
+            ((LANES, OWNERS * LANES), bf16),
+        ],
         [pltpu.VMEM((3, FACTS_HERE), jnp.int32), pltpu.SemaphoreType.DMA((3,))],
         [pl.BlockSpec(memory_space=pltpu.SMEM)] + [in_hbm] * 3,
     )(core, bucket, row_index, labels)
@@ -318,7 +367,7 @@
         pack_kernel,
         [((CHIPS, BLOCK_ROWS, LANES), f32), ((DIM_ROWS, LANES), f32), ((OWNERS, LANES), f32)],
         [pltpu.VMEM((3 * OWNERS, FACTS_HERE), bf16)],
-    )(partial, place, meta)
+    )(partial, place, meta, rank_hits)
     blocks = exchange(
         blocks, "rows", [[2 * chip + core for chip in range(CHIPS)] for core in range(2)]
     )
@@ -328,12 +377,24 @@
         [((1, FACTS_HERE), f32), ((DIM_ROWS, LANES), f32)],
         HALF_SCRATCH,
         flops=1 << 31,
-    )(blocks, dims, facts, meta, place)
+    )(blocks, dims, facts, meta, place, rank_hits, row_hits)
     grads, prob = call(
         grads_kernel,
         [((OWNERS, 2, LANES), f32), ((1, FACTS_HERE), f32)],
         HALF_SCRATCH,
-    )(other_blocks, dims, facts, meta, place, prob_half, sums_half, fact_table, dim_table)
+    )(
+        other_blocks,
+        dims,
+        facts,
+        meta,
+        place,
+        rank_hits,
+        row_hits,
+        prob_half,
+        sums_half,
+        fact_table,
+        dim_table,
+    )
     grads = exchange(grads, "rows")
     new_fact, new_dim = call(update_kernel, [((1, LANES), f32), ((1, LANES), f32)])(
         grads, fact_weight, dim_weight

time: 55.3 us -> 55 us (level)
  local copies, waits for them, and re-layouts: 0.81 us -> 1.45 us
  Pallas kernels: 7.32 us -> 6.69 us
    unnamed x14, local copies, waits for them, and re-layouts: 0.81 us -> 1.45 us
  transfers between devices with their start and end apart: 2 -> 2, of which waited for: 2 -> 2; matrix products, arithmetic and copies ran while one was open for 0% -> 0% of each run, Pallas kernels for 3% -> 4%
where the time goes in v3:
time: 55 us; the launch traced here: 54.6 us
  blocking collectives  25.4 us (46%)
  starting transfers between devices  13 us (24%)
  waiting for transfers between devices  7.39 us (13%)
  Pallas kernels  6.69 us (12%)
  local copies, waits for them, and re-layouts  1.45 us (3%)
  between operations  0.72 us (1%)
    all_to_all x2, blocking collectives, exchange(): lax.all_to_all(value, axis, split_axis=0, concat_axis=0, tiled=True, axis...  25.4 us
    all_to_all x1, starting transfers between devices, exchange(): lax.all_to_all(value, axis, split_axis=0, concat_axis=0, tiled=True, axis...  9.03 us
    all_to_all x1, waiting for transfers between devices, exchange(): lax.all_to_all(value, axis, split_axis=0, concat_axis=0, tiled=True, axis...  7.02 us
    ppermute x1, starting transfers between devices, shards(): lax.ppermute(blocks, 'rows', [(i, i ^ 1) for i in range(OWNERS)])  3.96 us
    pallas_call x1, Pallas kernels, shards(): call(scores_kernel, [((PEERS, SCORE_ROWS, LANES), f32)], [pltpu.VMEM(fact...  2.49 us
    unnamed x14, local copies, waits for them, and re-layouts  1.45 us
    pallas_call x1, Pallas kernels, shards(): call(grads_kernel, [((OWNERS, 2, LANES), f32), ((1, FACTS_HERE), f32)], H...  1.4 us
  transfers between devices with their start and end apart: 2, of which 2 were waited for; matrix products, arithmetic and copies ran while one was open for 0% of the time, Pallas kernels for 4%

profile of v3, /device:TPU:1, one launch (start us, length us, event | category | flops | bytes accessed | tf_op | source)
XLA Modules:
  0.0 54.6 jit_solution(4241310888502287461)
XLA Ops:
  0.6 0.0 copy-start.5
  0.6 0.0 copy-start.6
  0.7 0.6 %copy-done.5 = f32[128]{0:T(128)S(1)} copy-done((f32[128]{0:T(128)S(1)}, f32[128]{0:T(128)}, u32[]{:S(2)}) %copy-start.5) | copy-done | bytes 536
  1.3 0.0 copy-done.6
  1.3 2.5 %scores_kernel.1 = f32[8,48,128]{2,1,0:T(8,128)} custom-call(bf16[2048,128]{1,0:T(8,128)(2,1)} %fact_ref.1, bf16[4096,128]{1,0:T(8,128)(2,1)} %dim_ref.1, f32[1,128]{1,0:T(1,128)S(1)} %bitcast.12, f32[1,128]{1,0:T(1,128)S(1)} %bitcast.14), custom_call_target="tpu_custom_call" | custom-call | tf_op jit(solution)/shard_map/scores_kernel/pallas_call | solution.py:342
  3.8 0.0 copy-start.4
  3.8 9.0 %all-to-all-start = ((f32[8,48,128]{2,1,0:T(8,128)}), f32[8,48,128]{2,1,0:T(8,128)S(1)}, u32[]{:S(2)}, u32[]{:S(2)}) async-start(f32[8,48,128]{2,1,0:T(8,128)} %scores_kernel.1), calls=%async_computation | async-start | bytes 393216 | tf_op jit(solution)/shard_map/all_to_all | solution.py:328
  12.8 0.0 copy-start.3
  12.8 0.0 copy-start.2
  12.9 0.0 copy-done.4
  12.9 0.7 %copy-done.3 = s32[2048]{0:T(1024)S(1)} copy-done((s32[2048]{0:T(1024)S(1)}, s32[2048]{0:T(1024)}, u32[]{:S(2)}) %copy-start.3) | copy-done | bytes 8216
  13.5 0.0 copy-done.2
  13.6 1.1 %slots_kernel.1 = (s32[1,2048]{1,0:T(1,128)S(1)}, f32[32,128]{1,0:T(8,128)S(1)}, bf16[128,2048]{1,0:T(8,128)(2,1)S(1)}, bf16[128,4096]{1,0:T(8,128)(2,1)S(1)}) custom-call(s32[1]{0:T(128)} %bitcast.2.core_ref, s32[1,2048]{1,0:T(1,128)S(1)} %bitcast.9, s32[1,2048]{1,0:T(1,128)S(1)} %bitcast.10, s32[1,2048]{1,0:T(1,128)S(1)} %bitcast.11), custom_call_target="tpu_custom_call" | custom-call | tf_op jit(solution)/shard_map/slots_kernel/pallas_call | solution.py:354
  14.6 7.0 %all-to-all-done.recv_ref = f32[8,48,128]{2,1,0:T(8,128)S(1)} async-done(((f32[8,48,128]{2,1,0:T(8,128)}), f32[8,48,128]{2,1,0:T(8,128)S(1)}, u32[]{:S(2)}, u32[]{:S(2)}) %all-to-all-start) | async-done | bytes 196640 | tf_op jit(solution)/shard_map/all_to_all | solution.py:328
  21.7 0.3 pack_kernel.1
  22.0 14.3 %all_to_all.15.recv_ref = f32[16,36,128]{2,1,0:T(8,128)S(1)} all-to-all(f32[16,36,128]{2,1,0:T(8,128)S(1)} %get-tuple-element.19), channel_id=1, replica_groups={{0,16,32,48,64,80,96,112,128,144,160,176,192,208,224,240},{8,24,40,56,7..., dimensions={0} | all-to-all | bytes 589824 | tf_op jit(solution)/shard_map/all_to_all | solution.py:328
  36.3 4.0 %collective-permute-start = (f32[16,36,128]{2,1,0:T(8,128)S(1)}, f32[16,36,128]{2,1,0:T(8,128)S(1)}, u32[]{:S(2)}, u32[]{:S(2)}) collective-permute-start(f32[16,36,128]{2,1,0:T(8,128)S(1)} %all_to_all.15.recv_ref), channel_id=1, source_target_pairs={{0,8},{8,0},{16,24},{24,16},{32,40},{40,32},{48,56},{56,48},{64,72... | collective-permute-start | bytes 884744 | tf_op jit(solution)/shard_map/ppermute | solution.py:374
  40.2 0.0 copy-start
  40.2 0.0 copy-start.1
  40.2 0.9 %same_core_kernel.1 = (f32[1,2048]{1,0:T(1,128)S(1)}, f32[32,128]{1,0:T(8,128)S(1)}) custom-call(f32[16,36,128]{2,1,0:T(8,128)S(1)} %all_to_all.15.recv_ref, f32[32,128]{1,0:T(8,128)S(1)} %get-tuple-element.20.dims_ref, f32[32,128]{1,0:T(8,128)S(1)} %get-tuple-element.21.facts_ref, f32[32,128]{1,0:T(8,128)S(1)} %get-tuple-element.17.meta_ref, ...), custom_call_target="tpu_custom_call" | custom-call | flops 2147483648 | bytes 1048576 | tf_op jit(solution)/shard_map/same_core_kernel/pallas_call | solution.py:375
  41.1 0.4 collective-permute-done.recv_ref
  41.5 0.0 copy-done
  41.5 0.1 copy-done.1
  41.6 1.4 %grads_kernel.1 = (f32[32,2,128]{2,1,0:T(2,128)S(1)}, f32[1,2048]{1,0:T(1,128)}) custom-call(f32[16,36,128]{2,1,0:T(8,128)S(1)} %collective-permute-done.recv_ref, f32[32,128]{1,0:T(8,128)S(1)} %get-tuple-element.20.dims_ref, f32[32,128]{1,0:T(8,128)S(1)} %get-tuple-element.21.facts_ref, f32[32,128]{1,0:T(8,128)S(1)} %get-tuple-element.17.meta_ref, ...), custom_call_target="tpu_custom_call" | custom-call | tf_op jit(solution)/shard_map/grads_kernel/pallas_call | solution.py:381
  43.0 11.1 %all_to_all.16.recv_ref = f32[32,2,128]{2,1,0:T(2,128)S(1)} all-to-all(f32[32,2,128]{2,1,0:T(2,128)S(1)} %get-tuple-element.25), channel_id=1, replica_groups=mesh['rows'=32,'feat'=8] {'rows'}, dimensions={0} | all-to-all | bytes 65536 | tf_op jit(solution)/shard_map/all_to_all | solution.py:328
  54.1 0.6 %update_kernel.1 = (f32[1,128]{1,0:T(1,128)}, f32[1,128]{1,0:T(1,128)}) custom-call(f32[32,2,128]{2,1,0:T(2,128)S(1)} %all_to_all.16.recv_ref, f32[1,128]{1,0:T(1,128)S(1)} %bitcast.13, f32[1,128]{1,0:T(1,128)S(1)} %bitcast.15), custom_call_target="tpu_custom_call" | custom-call | tf_op jit(solution)/shard_map/update_kernel/pallas_call | solution.py:399
Async XLA Ops:
  0.6 0.7 %copy-start.5 = (f32[128]{0:T(128)S(1)}, f32[128]{0:T(128)}, u32[]{:S(2)}) copy-start(f32[128]{0:T(128)} %param.9) | copy-start | bytes 1540
  0.6 0.7 %copy-start.6 = (f32[128]{0:T(128)S(1)}, f32[128]{0:T(128)}, u32[]{:S(2)}) copy-start(f32[128]{0:T(128)} %param.10) | copy-start | bytes 1540
  3.8 9.1 %copy-start.4 = (s32[2048]{0:T(1024)S(1)}, s32[2048]{0:T(1024)}, u32[]{:S(2)}) copy-start(s32[2048]{0:T(1024)} %param.13) | copy-start | bytes 24580
  3.8 17.8 %all-to-all-start = ((f32[8,48,128]{2,1,0:T(8,128)}), f32[8,48,128]{2,1,0:T(8,128)S(1)}, u32[]{:S(2)}, u32[]{:S(2)}) async-start(f32[8,48,128]{2,1,0:T(8,128)} %scores_kernel.1), calls=%async_computation | async-start | bytes 393216 | tf_op jit(solution)/shard_map/all_to_all | solution.py:328
  12.8 0.7 %copy-start.3 = (s32[2048]{0:T(1024)S(1)}, s32[2048]{0:T(1024)}, u32[]{:S(2)}) copy-start(s32[2048]{0:T(1024)} %param.12) | copy-start | bytes 24580
  12.8 0.7 %copy-start.2 = (s32[2048,1]{0,1:T(1,128)S(1)}, s32[2048,1]{0,1:T(1,128)}, u32[]{:S(2)}) copy-start(s32[2048,1]{0,1:T(1,128)} %param.11) | copy-start | bytes 24580
  36.3 5.2 %collective-permute-start = (f32[16,36,128]{2,1,0:T(8,128)S(1)}, f32[16,36,128]{2,1,0:T(8,128)S(1)}, u32[]{:S(2)}, u32[]{:S(2)}) collective-permute-start(f32[16,36,128]{2,1,0:T(8,128)S(1)} %all_to_all.15.recv_ref), channel_id=1, source_target_pairs={{0,8},{8,0},{16,24},{24,16},{32,40},{40,32},{48,56},{56,48},{64,72... | collective-permute-start | bytes 884744 | tf_op jit(solution)/shard_map/ppermute | solution.py:374
  40.2 1.3 %copy-start = (bf16[4096,128]{1,0:T(8,128)(2,1)S(1)}, bf16[4096,128]{1,0:T(8,128)(2,1)}, u32[]{:S(2)}) copy-start(bf16[4096,128]{1,0:T(8,128)(2,1)} %dim_ref.1) | copy-start | bytes 3145732
  40.2 1.4 %copy-start.1 = (bf16[2048,128]{1,0:T(8,128)(2,1)S(1)}, bf16[2048,128]{1,0:T(8,128)(2,1)}, u32[]{:S(2)}) copy-start(bf16[2048,128]{1,0:T(8,128)(2,1)} %fact_ref.1) | copy-start | bytes 1572868

commit v4 on v3

--- a/solution.py
+++ b/solution.py
@@ -308,7 +308,7 @@
 ]
 
 
-def call(kernel, outs, scratch=(), in_specs=None, flops=None, vmem=32 << 20):
+def call(kernel, outs, scratch=(), in_specs=None, flops=None):
     extra = {} if in_specs is None else {"in_specs": in_specs}
     if flops is not None:
         extra["cost_estimate"] = pl.CostEstimate(
@@ -317,9 +317,9 @@
     return pl.pallas_call(
         kernel,
         name=kernel.__name__,
-        out_shape=[jax.ShapeDtypeStruct(shape, dtype) for shape, dtype in outs],
+        out_shape=outs,
         scratch_shapes=list(scratch),
-        compiler_params=pltpu.CompilerParams(vmem_limit_bytes=vmem),
+        compiler_params=pltpu.CompilerParams(vmem_limit_bytes=32 << 20),
         **extra,
     )
 
@@ -339,9 +339,12 @@
     core = (lax.axis_index("rows") & 1).reshape(1)
     in_hbm = pl.BlockSpec(memory_space=pltpu.HBM)
 
+    def stay(array):
+        return pltpu.with_memory_space_constraint(array, pltpu.HBM)
+
     (partial,) = call(
         scores_kernel,
-        [((PEERS, SCORE_ROWS, LANES), f32)],
+        [pltpu.VMEM((PEERS, SCORE_ROWS, LANES), f32)],
         [
             pltpu.VMEM(fact_table.shape, bf16),
             pltpu.VMEM(dim_table.shape, bf16),
@@ -349,23 +352,26 @@
             pltpu.SemaphoreType.DMA((2 + (len(fact_table) + len(dim_table)) // PIECE,)),
         ],
         [in_hbm] * 4,
-        vmem=(53 << 20) + (1 << 19),
-    )(fact_table, dim_table, fact_weight, dim_weight)
+    )(*[stay(array) for array in (fact_table, dim_table, fact_weight, dim_weight)])
     place, meta, rank_hits, row_hits = call(
         slots_kernel,
         [
-            ((1, FACTS_HERE), jnp.int32),
-            ((OWNERS, LANES), f32),
-            ((LANES, FACTS_HERE), bf16),
-            ((LANES, OWNERS * LANES), bf16),
+            pltpu.VMEM((1, FACTS_HERE), jnp.int32),
+            pltpu.VMEM((OWNERS, LANES), f32),
+            pltpu.VMEM((LANES, FACTS_HERE), bf16),
+            pltpu.VMEM((LANES, OWNERS * LANES), bf16),
         ],
         [pltpu.VMEM((3, FACTS_HERE), jnp.int32), pltpu.SemaphoreType.DMA((3,))],
         [pl.BlockSpec(memory_space=pltpu.SMEM)] + [in_hbm] * 3,
-    )(core, bucket, row_index, labels)
+    )(core, *[stay(array) for array in (bucket, row_index, labels)])
     partial = exchange(partial, "feat")
     blocks, dims, facts = call(
         pack_kernel,
-        [((CHIPS, BLOCK_ROWS, LANES), f32), ((DIM_ROWS, LANES), f32), ((OWNERS, LANES), f32)],
+        [
+            pltpu.VMEM((CHIPS, BLOCK_ROWS, LANES), f32),
+            pltpu.VMEM((DIM_ROWS, LANES), f32),
+            pltpu.VMEM((OWNERS, LANES), f32),
+        ],
         [pltpu.VMEM((3 * OWNERS, FACTS_HERE), bf16)],
     )(partial, place, meta, rank_hits)
     blocks = exchange(
@@ -374,13 +380,16 @@
     other_blocks = lax.ppermute(blocks, "rows", [(i, i ^ 1) for i in range(OWNERS)])
     prob_half, sums_half = call(
         same_core_kernel,
-        [((1, FACTS_HERE), f32), ((DIM_ROWS, LANES), f32)],
+        [pltpu.VMEM((1, FACTS_HERE), f32), pltpu.VMEM((DIM_ROWS, LANES), f32)],
         HALF_SCRATCH,
         flops=1 << 31,
     )(blocks, dims, facts, meta, place, rank_hits, row_hits)
     grads, prob = call(
         grads_kernel,
-        [((OWNERS, 2, LANES), f32), ((1, FACTS_HERE), f32)],
+        [
+            pltpu.VMEM((OWNERS, 2, LANES), f32),
+            jax.ShapeDtypeStruct((1, FACTS_HERE), f32),
+        ],
         HALF_SCRATCH,
     )(
         other_blocks,
@@ -396,7 +405,7 @@
         dim_table,
     )
     grads = exchange(grads, "rows")
-    new_fact, new_dim = call(update_kernel, [((1, LANES), f32), ((1, LANES), f32)])(
+    new_fact, new_dim = call(update_kernel, [jax.ShapeDtypeStruct((1, LANES), f32)] * 2)(
         grads, fact_weight, dim_weight
     )
     return new_fact.reshape(-1), new_dim.reshape(-1), prob.reshape(-1)

time: 55 us -> 54.3 us (0.987)
  local copies, waits for them, and re-layouts: 1.45 us -> 0.12 us
  Pallas kernels: 6.69 us -> 7.41 us
    unnamed x14 -> x8, local copies, waits for them, and re-layouts: 1.45 us -> 0.12 us
    pallas_call x6, Pallas kernels: 6.69 us -> 7.41 us  [the longest x1 2.52 us: shards(): call(scores_kernel, [pltpu.VMEM((PEERS, SCORE_ROWS, LANES), f32)], [pltpu...]
  transfers between devices with their start and end apart: 2 -> 2, of which waited for: 2 -> 2; matrix products, arithmetic and copies ran while one was open for 0% -> 0% of each run, Pallas kernels for 4% -> 5%
where the time goes in v4:
time: 54.3 us; the launch traced here: 54 us
  blocking collectives  25.4 us (47%)
  starting transfers between devices  13 us (24%)
  waiting for transfers between devices  7.42 us (14%)
  Pallas kernels  7.41 us (14%)
  between operations  0.69 us (1%)
    all_to_all x2, blocking collectives, exchange(): lax.all_to_all(value, axis, split_axis=0, concat_axis=0, tiled=True, axis...  25.4 us
    all_to_all x1, starting transfers between devices, exchange(): lax.all_to_all(value, axis, split_axis=0, concat_axis=0, tiled=True, axis...  9.03 us
    all_to_all x1, waiting for transfers between devices, exchange(): lax.all_to_all(value, axis, split_axis=0, concat_axis=0, tiled=True, axis...  7.05 us
    ppermute x1, starting transfers between devices, shards(): lax.ppermute(blocks, 'rows', [(i, i ^ 1) for i in range(OWNERS)])  3.96 us
    pallas_call x1, Pallas kernels, shards(): call(scores_kernel, [pltpu.VMEM((PEERS, SCORE_ROWS, LANES), f32)], [pltpu...  2.52 us
    pallas_call x1, Pallas kernels, shards(): call(slots_kernel, [pltpu.VMEM((1, FACTS_HERE), jnp.int32), pltpu.VMEM((O...  1.76 us
    pallas_call x1, Pallas kernels, shards(): call(grads_kernel, [pltpu.VMEM((OWNERS, 2, LANES), f32), jax.ShapeDtypeSt...  1.41 us
  transfers between devices with their start and end apart: 2, of which 2 were waited for; matrix products, arithmetic and copies ran while one was open for 0% of the time, Pallas kernels for 5%

profile of v4, /device:TPU:1, one launch (start us, length us, event | category | flops | bytes accessed | tf_op | source)
XLA Modules:
  0.0 54.0 jit_solution(9287352332583549782)
XLA Ops:
  0.6 2.5 %scores_kernel.1 = f32[8,48,128]{2,1,0:T(8,128)} custom-call(bf16[2048,128]{1,0:T(8,128)(2,1)} %fact_ref.1, bf16[4096,128]{1,0:T(8,128)(2,1)} %dim_ref.1, f32[1,128]{1,0:T(1,128)} %bitcast.9, f32[1,128]{1,0:T(1,128)} %bitcast.11), custom_call_target="tpu_custom_call" | custom-call | tf_op jit(solution)/shard_map/scores_kernel/pallas_call | solution.py:345
  3.2 9.0 %all-to-all-start = ((f32[8,48,128]{2,1,0:T(8,128)}), f32[8,48,128]{2,1,0:T(8,128)S(1)}, u32[]{:S(2)}, u32[]{:S(2)}) async-start(f32[8,48,128]{2,1,0:T(8,128)} %scores_kernel.1), calls=%async_computation | async-start | bytes 393216 | tf_op jit(solution)/shard_map/all_to_all | solution.py:328
  12.2 1.8 %slots_kernel.1 = (s32[1,2048]{1,0:T(1,128)S(1)}, f32[32,128]{1,0:T(8,128)S(1)}, bf16[128,2048]{1,0:T(8,128)(2,1)S(1)}, bf16[128,4096]{1,0:T(8,128)(2,1)S(1)}) custom-call(s32[1]{0:T(128)} %bitcast.2.core_ref, s32[1,2048]{1,0:T(1,128)} %bitcast.13, s32[1,2048]{1,0:T(1,128)} %bitcast.14, s32[1,2048]{1,0:T(1,128)} %bitcast.15), custom_call_target="tpu_custom_call" | custom-call | tf_op jit(solution)/shard_map/slots_kernel/pallas_call | solution.py:356
  13.9 7.0 %all-to-all-done.recv_ref = f32[8,48,128]{2,1,0:T(8,128)S(1)} async-done(((f32[8,48,128]{2,1,0:T(8,128)}), f32[8,48,128]{2,1,0:T(8,128)S(1)}, u32[]{:S(2)}, u32[]{:S(2)}) %all-to-all-start) | async-done | bytes 196640 | tf_op jit(solution)/shard_map/all_to_all | solution.py:328
  21.0 0.3 pack_kernel.1
  21.3 14.3 %all_to_all.15.recv_ref = f32[16,36,128]{2,1,0:T(8,128)S(1)} all-to-all(f32[16,36,128]{2,1,0:T(8,128)S(1)} %get-tuple-element.19), channel_id=1, replica_groups={{0,16,32,48,64,80,96,112,128,144,160,176,192,208,224,240},{8,24,40,56,7..., dimensions={0} | all-to-all | bytes 589824 | tf_op jit(solution)/shard_map/all_to_all | solution.py:328
  35.6 4.0 %collective-permute-start = (f32[16,36,128]{2,1,0:T(8,128)S(1)}, f32[16,36,128]{2,1,0:T(8,128)S(1)}, u32[]{:S(2)}, u32[]{:S(2)}) collective-permute-start(f32[16,36,128]{2,1,0:T(8,128)S(1)} %all_to_all.15.recv_ref), channel_id=1, source_target_pairs={{0,8},{8,0},{16,24},{24,16},{32,40},{40,32},{48,56},{56,48},{64,72... | collective-permute-start | bytes 884744 | tf_op jit(solution)/shard_map/ppermute | solution.py:380
  39.6 0.0 copy-start
  39.6 0.0 copy-start.1
  39.6 0.9 %same_core_kernel.1 = (f32[1,2048]{1,0:T(1,128)S(1)}, f32[32,128]{1,0:T(8,128)S(1)}) custom-call(f32[16,36,128]{2,1,0:T(8,128)S(1)} %all_to_all.15.recv_ref, f32[32,128]{1,0:T(8,128)S(1)} %get-tuple-element.20.dims_ref, f32[32,128]{1,0:T(8,128)S(1)} %get-tuple-element.21.facts_ref, f32[32,128]{1,0:T(8,128)S(1)} %get-tuple-element.17.meta_ref, ...), custom_call_target="tpu_custom_call" | custom-call | flops 2147483648 | bytes 1048576 | tf_op jit(solution)/shard_map/same_core_kernel/pallas_call | solution.py:381
  40.5 0.4 collective-permute-done.recv_ref
  40.8 0.0 copy-done
  40.8 0.1 copy-done.1
  40.9 1.4 %grads_kernel.1 = (f32[32,2,128]{2,1,0:T(2,128)S(1)}, f32[1,2048]{1,0:T(1,128)}) custom-call(f32[16,36,128]{2,1,0:T(8,128)S(1)} %collective-permute-done.recv_ref, f32[32,128]{1,0:T(8,128)S(1)} %get-tuple-element.20.dims_ref, f32[32,128]{1,0:T(8,128)S(1)} %get-tuple-element.21.facts_ref, f32[32,128]{1,0:T(8,128)S(1)} %get-tuple-element.17.meta_ref, ...), custom_call_target="tpu_custom_call" | custom-call | tf_op jit(solution)/shard_map/grads_kernel/pallas_call | solution.py:387
  42.4 0.0 copy-start.2
  42.4 0.0 copy-start.3
  42.4 11.1 %all_to_all.16.recv_ref = f32[32,2,128]{2,1,0:T(2,128)S(1)} all-to-all(f32[32,2,128]{2,1,0:T(2,128)S(1)} %get-tuple-element.25), channel_id=1, replica_groups=mesh['rows'=32,'feat'=8] {'rows'}, dimensions={0} | all-to-all | bytes 65536 | tf_op jit(solution)/shard_map/all_to_all | solution.py:328
  53.5 0.0 copy-done.2
  53.5 0.0 copy-done.3
  53.5 0.6 %update_kernel.1 = (f32[1,128]{1,0:T(1,128)}, f32[1,128]{1,0:T(1,128)}) custom-call(f32[32,2,128]{2,1,0:T(2,128)S(1)} %all_to_all.16.recv_ref, f32[1,128]{1,0:T(1,128)S(1)} %bitcast.10, f32[1,128]{1,0:T(1,128)S(1)} %bitcast.12), custom_call_target="tpu_custom_call" | custom-call | tf_op jit(solution)/shard_map/update_kernel/pallas_call | solution.py:408
Async XLA Ops:
  3.2 17.8 %all-to-all-start = ((f32[8,48,128]{2,1,0:T(8,128)}), f32[8,48,128]{2,1,0:T(8,128)S(1)}, u32[]{:S(2)}, u32[]{:S(2)}) async-start(f32[8,48,128]{2,1,0:T(8,128)} %scores_kernel.1), calls=%async_computation | async-start | bytes 393216 | tf_op jit(solution)/shard_map/all_to_all | solution.py:328
  35.6 5.2 %collective-permute-start = (f32[16,36,128]{2,1,0:T(8,128)S(1)}, f32[16,36,128]{2,1,0:T(8,128)S(1)}, u32[]{:S(2)}, u32[]{:S(2)}) collective-permute-start(f32[16,36,128]{2,1,0:T(8,128)S(1)} %all_to_all.15.recv_ref), channel_id=1, source_target_pairs={{0,8},{8,0},{16,24},{24,16},{32,40},{40,32},{48,56},{56,48},{64,72... | collective-permute-start | bytes 884744 | tf_op jit(solution)/shard_map/ppermute | solution.py:380
  39.6 1.3 %copy-start = (bf16[4096,128]{1,0:T(8,128)(2,1)S(1)}, bf16[4096,128]{1,0:T(8,128)(2,1)}, u32[]{:S(2)}) copy-start(bf16[4096,128]{1,0:T(8,128)(2,1)} %dim_ref.1) | copy-start | bytes 3145732
  39.6 1.4 %copy-start.1 = (bf16[2048,128]{1,0:T(8,128)(2,1)S(1)}, bf16[2048,128]{1,0:T(8,128)(2,1)}, u32[]{:S(2)}) copy-start(bf16[2048,128]{1,0:T(8,128)(2,1)} %fact_ref.1) | copy-start | bytes 1572868
  42.4 11.1 %copy-start.2 = (f32[128]{0:T(128)S(1)}, f32[128]{0:T(128)}, u32[]{:S(2)}) copy-start(f32[128]{0:T(128)} %param.9) | copy-start | bytes 1540
  42.4 11.1 %copy-start.3 = (f32[128]{0:T(128)S(1)}, f32[128]{0:T(128)}, u32[]{:S(2)}) copy-start(f32[128]{0:T(128)} %param.10) | copy-start | bytes 1540

commit v5 on v4

--- a/solution.py
+++ b/solution.py
@@ -56,56 +56,7 @@
     return jnp.where(hits(row, count), 1.0, 0.0).astype(bf16)
 
 
-def scores_kernel(
-    fact_hbm, dim_hbm, fact_weight_hbm, dim_weight_hbm, out_ref, fact, dim, weights, sems
-):
-    def copies(source, target, first):
-        found = []
-        for i in range(source.shape[0] // PIECE):
-            cut = pl.ds(i * PIECE, PIECE)
-            found.append(pltpu.make_async_copy(source.at[cut], target.at[cut], sems.at[first + i]))
-        return found
-
-    dim_pieces = copies(dim_hbm, dim, 2)
-    fact_pieces = copies(fact_hbm, fact, 2 + len(dim_pieces))
-    dim_weight = pltpu.make_async_copy(dim_weight_hbm, weights.at[pl.ds(0, 1)], sems.at[0])
-    fact_weight = pltpu.make_async_copy(fact_weight_hbm, weights.at[pl.ds(1, 1)], sems.at[1])
-    for copy in [dim_weight, fact_weight] + fact_pieces + dim_pieces:
-        copy.start()
-    for row, place, weight, table, pieces in (
-        (DIM_ROWS, 1, fact_weight, fact, fact_pieces),
-        (0, 0, dim_weight, dim, dim_pieces),
-    ):
-        weight.wait()
-        for piece in pieces:
-            piece.wait()
-        part = dot_nt(stacked_row(weights[place : place + 1, :]), table[...])
-        part = jnp.sum(part, 0, keepdims=True)
-        for i in range(table.shape[0] // LANES):
-            out_ref[0, row : row + 1, :] = part[:, i * LANES : (i + 1) * LANES]
-            row += 1
-    for peer in range(1, PEERS):
-        out_ref[peer] = out_ref[0]
-
-
-def slots_kernel(
-    core_ref,
-    bucket_hbm,
-    index_hbm,
-    label_hbm,
-    place_ref,
-    meta_ref,
-    rank_hits_ref,
-    row_hits_ref,
-    given,
-    sems,
-):
-    loads = [
-        pltpu.make_async_copy(source, given.at[pl.ds(i, 1)], sems.at[i])
-        for i, source in enumerate((bucket_hbm, index_hbm, label_hbm))
-    ]
-    for load in loads:
-        load.start()
+def place_facts(core, bucket, index, label, place_ref, meta_ref, rank_hits_ref):
     width = 2 * LANES
     chunks = FACTS_HERE // width
     upto = jnp.where(
@@ -114,11 +65,7 @@
         1.0,
         0.0,
     ).astype(bf16)
-    for load in loads:
-        load.wait()
-    bucket = given[0:1, :]
-    owner = (bucket >> 1) + ((bucket & 1) ^ core_ref[0]) * CHIPS
-    label = given[2:3, :]
+    owner = (bucket >> 1) + ((bucket & 1) ^ core) * CHIPS
     owner_hits = onehot(owner, OWNERS)
     stack = jnp.concatenate(
         [owner_hits[:, c * width : (c + 1) * width] for c in range(chunks)], 0
@@ -133,7 +80,6 @@
         before = before + here[:, width - 1 : width]
     rank = jnp.concatenate(ranks, 1).astype(jnp.int32) - 1
     place_ref[...] = owner + (label << LABEL_BIT)
-    index = given[1:2, :]
     low = (index & (LANES - 1)).astype(f32)
     high = ((index >> 7) + (label << (LABEL_BIT - 7)) + (1 << (VALID_BIT - 7))).astype(f32)
     mine = hits(owner, OWNERS)
@@ -142,10 +88,68 @@
     rank_hits_ref[...] = rank_hits
     packed = dot_nt(fields.astype(bf16), rank_hits)
     meta_ref[...] = packed[:OWNERS] + packed[OWNERS:] * LANES
-    low = packed[:OWNERS].astype(jnp.int32)
-    for owner in range(OWNERS):
-        cut = slice(owner * LANES, (owner + 1) * LANES)
-        row_hits_ref[:, cut] = onehot(low[owner : owner + 1], LANES)
+
+
+def prepare_kernel(
+    core_ref,
+    bucket_hbm,
+    index_hbm,
+    label_hbm,
+    fact_hbm,
+    dim_hbm,
+    fact_weight_hbm,
+    dim_weight_hbm,
+    out_ref,
+    place_ref,
+    meta_ref,
+    rank_hits_ref,
+    given,
+    weights,
+    table,
+    sems,
+):
+    loads = [
+        pltpu.make_async_copy(source, given.at[pl.ds(i, 1)], sems.at[i])
+        for i, source in enumerate((bucket_hbm, index_hbm, label_hbm))
+    ] + [
+        pltpu.make_async_copy(source, weights.at[pl.ds(i, 1)], sems.at[3 + i])
+        for i, source in enumerate((fact_weight_hbm, dim_weight_hbm))
+    ]
+    pieces = []
+    for first, source in ((0, dim_hbm), (dim_hbm.shape[0], fact_hbm)):
+        for start in range(0, source.shape[0], PIECE):
+            pieces.append(
+                pltpu.make_async_copy(
+                    source.at[pl.ds(start, PIECE)],
+                    table.at[pl.ds(first + start, PIECE)],
+                    sems.at[len(loads) + len(pieces)],
+                )
+            )
+    for copy in loads + pieces:
+        copy.start()
+    for load in loads:
+        load.wait()
+    place_facts(
+        core_ref[0],
+        given[0:1, :],
+        given[1:2, :],
+        given[2:3, :],
+        place_ref,
+        meta_ref,
+        rank_hits_ref,
+    )
+    terms = jnp.concatenate([stacked_row(weights[i : i + 1, :]) for i in range(2)], 0)
+    for copy in pieces:
+        copy.wait()
+    parts = dot_nt(terms, table[...])
+    for start, rows in ((8, range(DIM_ROWS)), (0, range(DIM_ROWS, SCORE_ROWS))):
+        part = jnp.sum(
+            parts[start : start + 8, rows[0] * LANES : (rows[-1] + 1) * LANES], 0, keepdims=True
+        )
+        for i, row in enumerate(rows):
+            out_ref[0, row : row + 1, :] = part[:, i * LANES : (i + 1) * LANES]
+    for peer in range(1, PEERS):
+        out_ref[peer] = out_ref[0]
 
 
 def places(place_ref):
@@ -204,13 +208,12 @@
     meta = meta_ref[slots, :].astype(jnp.int32)
     dims = stacked(dims_ref[...])
     for chip in range(CHIPS):
-        cut = slice((other * CHIPS + chip) * LANES, (other * CHIPS + chip + 1) * LANES)
+        cut = slice(chip * LANES, (chip + 1) * LANES)
         parts = dot_nn(stacked(recv_ref[chip, :DIM_ROWS, :]), row_hits_ref[:, cut])
         home_ref[chip : chip + 1, :] = taken(
             summed(parts, DIM_ROWS), (meta[chip : chip + 1] >> 7) & (DIM_ROWS - 1)
         )
         row = DIM_ROWS + other
-        cut = slice(chip * LANES, (chip + 1) * LANES)
         code = recv_ref[chip, row + 2 : row + 3, :].astype(jnp.int32)
         code_ref[chip : chip + 1, :] = code
         column = onehot(code & (LANES - 1), LANES)
@@ -244,14 +247,22 @@
     meta_ref,
     place_ref,
     rank_hits_ref,
-    row_hits_ref,
     prob_ref,
     sums_ref,
+    row_hits_ref,
+    here_ref,
     *scratch,
 ):
+    meta = meta_ref[...].astype(jnp.int32) & (LANES - 1)
+    for chip in range(CHIPS):
+        cut = slice(chip * LANES, (chip + 1) * LANES)
+        here_ref[:, cut] = onehot(meta[chip : chip + 1], LANES)
     prob_ref[...], sums_ref[...] = half(
-        0, recv_ref, dims_ref, facts_ref, meta_ref, place_ref, rank_hits_ref, row_hits_ref, scratch
-    )
+        0, recv_ref, dims_ref, facts_ref, meta_ref, place_ref, rank_hits_ref, here_ref, scratch
+    )
+    for chip in range(CHIPS):
+        cut = slice(chip * LANES, (chip + 1) * LANES)
+        row_hits_ref[:, cut] = onehot(meta[CHIPS + chip : CHIPS + chip + 1], LANES)
 
 
 def grads_kernel(
@@ -337,33 +348,37 @@
     fact_weight = fact_weight.reshape(1, LANES)
     dim_weight = dim_weight.reshape(1, LANES)
     core = (lax.axis_index("rows") & 1).reshape(1)
-    in_hbm = pl.BlockSpec(memory_space=pltpu.HBM)
-
-    def stay(array):
-        return pltpu.with_memory_space_constraint(array, pltpu.HBM)
-
-    (partial,) = call(
-        scores_kernel,
-        [pltpu.VMEM((PEERS, SCORE_ROWS, LANES), f32)],
+    partial, place, meta, rank_hits = call(
+        prepare_kernel,
         [
-            pltpu.VMEM(fact_table.shape, bf16),
-            pltpu.VMEM(dim_table.shape, bf16),
-            pltpu.VMEM((2, LANES), f32),
-            pltpu.SemaphoreType.DMA((2 + (len(fact_table) + len(dim_table)) // PIECE,)),
-        ],
-        [in_hbm] * 4,
-    )(*[stay(array) for array in (fact_table, dim_table, fact_weight, dim_weight)])
-    place, meta, rank_hits, row_hits = call(
-        slots_kernel,
-        [
+            pltpu.VMEM((PEERS, SCORE_ROWS, LANES), f32),
             pltpu.VMEM((1, FACTS_HERE), jnp.int32),
             pltpu.VMEM((OWNERS, LANES), f32),
             pltpu.VMEM((LANES, FACTS_HERE), bf16),
-            pltpu.VMEM((LANES, OWNERS * LANES), bf16),
-        ],
-        [pltpu.VMEM((3, FACTS_HERE), jnp.int32), pltpu.SemaphoreType.DMA((3,))],
-        [pl.BlockSpec(memory_space=pltpu.SMEM)] + [in_hbm] * 3,
-    )(core, *[stay(array) for array in (bucket, row_index, labels)])
+        ],
+        [
+            pltpu.VMEM((3, FACTS_HERE), jnp.int32),
+            pltpu.VMEM((2, LANES), f32),
+            pltpu.VMEM((SCORE_ROWS * LANES, LANES), bf16),
+            pltpu.SemaphoreType.DMA((5 + (len(fact_table) + len(dim_table)) // PIECE,)),
+        ],
+        [pl.BlockSpec(memory_space=pltpu.SMEM)]
+        + [pl.BlockSpec(memory_space=pltpu.HBM)] * 7,
+    )(
+        core,
+        *[
+            pltpu.with_memory_space_constraint(array, pltpu.HBM)
+            for array in (
+                bucket,
+                row_index,
+                labels,
+                fact_table,
+                dim_table,
+                fact_weight,
+                dim_weight,
+            )
+        ],
+    )
     partial = exchange(partial, "feat")
     blocks, dims, facts = call(
         pack_kernel,
@@ -378,12 +393,16 @@
         blocks, "rows", [[2 * chip + core for chip in range(CHIPS)] for core in range(2)]
     )
     other_blocks = lax.ppermute(blocks, "rows", [(i, i ^ 1) for i in range(OWNERS)])
-    prob_half, sums_half = call(
+    prob_half, sums_half, row_hits = call(
         same_core_kernel,
-        [pltpu.VMEM((1, FACTS_HERE), f32), pltpu.VMEM((DIM_ROWS, LANES), f32)],
-        HALF_SCRATCH,
+        [
+            pltpu.VMEM((1, FACTS_HERE), f32),
+            pltpu.VMEM((DIM_ROWS, LANES), f32),
+            pltpu.VMEM((LANES, CHIPS * LANES), bf16),
+        ],
+        [pltpu.VMEM((LANES, CHIPS * LANES), bf16)] + HALF_SCRATCH,
         flops=1 << 31,
-    )(blocks, dims, facts, meta, place, rank_hits, row_hits)
+    )(blocks, dims, facts, meta, place, rank_hits)
     grads, prob = call(
         grads_kernel,
         [

time: 54.3 us -> 53.7 us (0.989)
  blocking collectives: 25.4 us -> 43 us
  starting transfers between devices: 13 us -> 3.96 us
  waiting for transfers between devices: 7.42 us -> 0.15 us
  Pallas kernels: 7.41 us -> 5.52 us
    all_to_all x2 -> x3, blocking collectives: 25.4 us -> 43 us  [exchange(): lax.all_to_all(value, axis, split_axis=0, concat_axis=0, tiled=True, axis...]
    all_to_all x1 -> x0, starting transfers between devices: 9.03 us -> none  [exchange(): lax.all_to_all(value, axis, split_axis=0, concat_axis=0, tiled=True, axis...]
    all_to_all x1 -> x0, waiting for transfers between devices: 7.05 us -> none  [exchange(): lax.all_to_all(value, axis, split_axis=0, concat_axis=0, tiled=True, axis...]
    pallas_call x2 -> x1, Pallas kernels: 4.27 us -> 2.15 us  [shards(): call(prepare_kernel, [pltpu.VMEM((PEERS, SCORE_ROWS, LANES), f32), pltpu....]
  transfers between devices with their start and end apart: 2 -> 1, of which waited for: 2 -> 1; matrix products, arithmetic and copies ran while one was open for 0% -> 0% of each run, Pallas kernels for 5% -> 2%
where the time goes in v5:
time: 53.7 us; the launch traced here: 53.4 us
  blocking collectives  43 us (80%)
  Pallas kernels  5.52 us (10%)
  starting transfers between devices  3.96 us (7%)
  between operations  0.7 us (1%)
    all_to_all x3, blocking collectives, exchange(): lax.all_to_all(value, axis, split_axis=0, concat_axis=0, tiled=True, axis...  43 us
    ppermute x1, starting transfers between devices, shards(): lax.ppermute(blocks, 'rows', [(i, i ^ 1) for i in range(OWNERS)])  3.96 us
    pallas_call x1, Pallas kernels, shards(): call(prepare_kernel, [pltpu.VMEM((PEERS, SCORE_ROWS, LANES), f32), pltpu....  2.15 us
    pallas_call x1, Pallas kernels, shards(): call(grads_kernel, [pltpu.VMEM((OWNERS, 2, LANES), f32), jax.ShapeDtypeSt...  1.41 us
    pallas_call x1, Pallas kernels, shards(): call(same_core_kernel, [pltpu.VMEM((1, FACTS_HERE), f32), pltpu.VMEM((DIM...  1.1 us
  transfers between devices with their start and end apart: 1, of which 1 were waited for; matrix products, arithmetic and copies ran while one was open for 0% of the time, Pallas kernels for 2%

profile of v5, /device:TPU:1, one launch (start us, length us, event | category | flops | bytes accessed | tf_op | source)
XLA Modules:
  0.0 53.4 jit_solution(16384911695338432743)
XLA Ops:
  0.6 2.2 %prepare_kernel.1 = (f32[8,48,128]{2,1,0:T(8,128)S(1)}, s32[1,2048]{1,0:T(1,128)S(1)}, f32[32,128]{1,0:T(8,128)S(1)}, bf16[128,2048]{1,0:T(8,128)(2,1)S(1)}) custom-call(s32[1]{0:T(128)} %bitcast.core_ref, s32[1,2048]{1,0:T(1,128)} %bitcast.13, s32[1,2048]{1,0:T(1,128)} %bitcast.14, s32[1,2048]{1,0:T(1,128)} %bitcast.15, bf16[2048,128]{1,0:T(8,128)(2,1)} %fact_ref.1, ...), custom_call_target="tpu_custom_call" | custom-call | tf_op jit(solution)/shard_map/prepare_kernel/pallas_call | solution.py:351
  2.8 17.6 %all_to_all.15.recv_ref = f32[8,48,128]{2,1,0:T(8,128)S(1)} all-to-all(f32[8,48,128]{2,1,0:T(8,128)S(1)} %get-tuple-element.17), channel_id=1, replica_groups=mesh['rows'=32,'feat'=8] {'feat'}, dimensions={0} | all-to-all | bytes 393216 | tf_op jit(solution)/shard_map/all_to_all | solution.py:339
  20.4 0.3 pack_kernel.1
  20.7 14.3 %all_to_all.16.recv_ref = f32[16,36,128]{2,1,0:T(8,128)S(1)} all-to-all(f32[16,36,128]{2,1,0:T(8,128)S(1)} %get-tuple-element.21), channel_id=1, replica_groups={{0,16,32,48,64,80,96,112,128,144,160,176,192,208,224,240},{8,24,40,56,7..., dimensions={0} | all-to-all | bytes 589824 | tf_op jit(solution)/shard_map/all_to_all | solution.py:339
  35.1 4.0 %collective-permute-start = (f32[16,36,128]{2,1,0:T(8,128)S(1)}, f32[16,36,128]{2,1,0:T(8,128)S(1)}, u32[]{:S(2)}, u32[]{:S(2)}) collective-permute-start(f32[16,36,128]{2,1,0:T(8,128)S(1)} %all_to_all.16.recv_ref), channel_id=1, source_target_pairs={{0,8},{8,0},{16,24},{24,16},{32,40},{40,32},{48,56},{56,48},{64,72... | collective-permute-start | bytes 884744 | tf_op jit(solution)/shard_map/ppermute | solution.py:395
  39.0 0.0 copy-start
  39.0 0.0 copy-start.1
  39.0 1.1 %same_core_kernel.1 = (f32[1,2048]{1,0:T(1,128)S(1)}, f32[32,128]{1,0:T(8,128)S(1)}, bf16[128,2048]{1,0:T(8,128)(2,1)S(1)}) custom-call(f32[16,36,128]{2,1,0:T(8,128)S(1)} %all_to_all.16.recv_ref, f32[32,128]{1,0:T(8,128)S(1)} %get-tuple-element.22.dims_ref, f32[32,128]{1,0:T(8,128)S(1)} %get-tuple-element.23.facts_ref, ...), custom_call_target="tpu_custom_call" | custom-call | flops 2147483648 | bytes 1048576 | tf_op jit(solution)/shard_map/same_core_kernel/pallas_call | solution.py:396
  40.1 0.1 collective-permute-done.recv_ref
  40.3 0.0 copy-done
  40.3 0.1 copy-done.1
  40.4 1.4 %grads_kernel.1 = (f32[32,2,128]{2,1,0:T(2,128)S(1)}, f32[1,2048]{1,0:T(1,128)}) custom-call(f32[16,36,128]{2,1,0:T(8,128)S(1)} %collective-permute-done.recv_ref, f32[32,128]{1,0:T(8,128)S(1)} %get-tuple-element.22.dims_ref, f32[32,128]{1,0:T(8,128)S(1)} %get-tuple-element.23.facts_ref, f32[32,128]{1,0:T(8,128)S(1)} %get-tuple-element.19.meta_ref, ...), custom_call_target="tpu_custom_call" | custom-call | tf_op jit(solution)/shard_map/grads_kernel/pallas_call | solution.py:406
  41.8 0.0 copy-start.2
  41.8 0.0 copy-start.3
  41.8 11.1 %all_to_all.17.recv_ref = f32[32,2,128]{2,1,0:T(2,128)S(1)} all-to-all(f32[32,2,128]{2,1,0:T(2,128)S(1)} %get-tuple-element.27), channel_id=1, replica_groups=mesh['rows'=32,'feat'=8] {'rows'}, dimensions={0} | all-to-all | bytes 65536 | tf_op jit(solution)/shard_map/all_to_all | solution.py:339
  52.9 0.0 copy-done.2
  52.9 0.0 copy-done.3
  52.9 0.6 %update_kernel.1 = (f32[1,128]{1,0:T(1,128)}, f32[1,128]{1,0:T(1,128)}) custom-call(f32[32,2,128]{2,1,0:T(2,128)S(1)} %all_to_all.17.recv_ref, f32[1,128]{1,0:T(1,128)S(1)} %bitcast.10, f32[1,128]{1,0:T(1,128)S(1)} %bitcast.12), custom_call_target="tpu_custom_call" | custom-call | tf_op jit(solution)/shard_map/update_kernel/pallas_call | solution.py:427
Async XLA Ops:
  35.1 5.2 %collective-permute-start = (f32[16,36,128]{2,1,0:T(8,128)S(1)}, f32[16,36,128]{2,1,0:T(8,128)S(1)}, u32[]{:S(2)}, u32[]{:S(2)}) collective-permute-start(f32[16,36,128]{2,1,0:T(8,128)S(1)} %all_to_all.16.recv_ref), channel_id=1, source_target_pairs={{0,8},{8,0},{16,24},{24,16},{32,40},{40,32},{48,56},{56,48},{64,72... | collective-permute-start | bytes 884744 | tf_op jit(solution)/shard_map/ppermute | solution.py:395
  39.0 1.3 %copy-start = (bf16[4096,128]{1,0:T(8,128)(2,1)S(1)}, bf16[4096,128]{1,0:T(8,128)(2,1)}, u32[]{:S(2)}) copy-start(bf16[4096,128]{1,0:T(8,128)(2,1)} %dim_ref.1) | copy-start | bytes 3145732
  39.0 1.4 %copy-start.1 = (bf16[2048,128]{1,0:T(8,128)(2,1)S(1)}, bf16[2048,128]{1,0:T(8,128)(2,1)}, u32[]{:S(2)}) copy-start(bf16[2048,128]{1,0:T(8,128)(2,1)} %fact_ref.1) | copy-start | bytes 1572868
  41.8 11.1 %copy-start.2 = (f32[128]{0:T(128)S(1)}, f32[128]{0:T(128)}, u32[]{:S(2)}) copy-start(f32[128]{0:T(128)} %param.9) | copy-start | bytes 1540
  41.8 11.1 %copy-start.3 = (f32[128]{0:T(128)S(1)}, f32[128]{0:T(128)}, u32[]{:S(2)}) copy-start(f32[128]{0:T(128)} %param.10) | copy-start | bytes 1540

commit v6 on v5

--- a/solution.py
+++ b/solution.py
@@ -56,7 +56,11 @@
     return jnp.where(hits(row, count), 1.0, 0.0).astype(bf16)
 
 
-def place_facts(core, bucket, index, label, place_ref, meta_ref, rank_hits_ref):
+def side_of(row):
+    return (row ^ (row >> 2)) & 1
+
+
+def place_facts(side, bucket, index, label, place_ref, meta_ref, rank_hits_ref):
     width = 2 * LANES
     chunks = FACTS_HERE // width
     upto = jnp.where(
@@ -65,7 +69,7 @@
         1.0,
         0.0,
     ).astype(bf16)
-    owner = (bucket >> 1) + ((bucket & 1) ^ core) * CHIPS
+    owner = (bucket >> 1) + (side_of(bucket) ^ side) * CHIPS
     owner_hits = onehot(owner, OWNERS)
     stack = jnp.concatenate(
         [owner_hits[:, c * width : (c + 1) * width] for c in range(chunks)], 0
@@ -91,7 +95,7 @@
 
 
 def prepare_kernel(
-    core_ref,
+    side_ref,
     bucket_hbm,
     index_hbm,
     label_hbm,
@@ -130,7 +134,7 @@
     for load in loads:
         load.wait()
     place_facts(
-        core_ref[0],
+        side_ref[0],
         given[0:1, :],
         given[1:2, :],
         given[2:3, :],
@@ -215,32 +219,28 @@
         )
         row = DIM_ROWS + other
         code = recv_ref[chip, row + 2 : row + 3, :].astype(jnp.int32)
-        code_ref[chip : chip + 1, :] = code
-        column = onehot(code & (LANES - 1), LANES)
-        low_ref[:, cut] = column
-        own_ref[chip : chip + 1, :] = recv_ref[chip, row : row + 1, :] + taken(
-            summed(dot_nn(dims, column), DIM_ROWS), (code >> 7) & (DIM_ROWS - 1)
-        )
+        code_ref[:, cut] = code
+        low_ref[:, cut] = onehot(code & (LANES - 1), LANES)
+        own_ref[:, cut] = recv_ref[chip, row : row + 1, :]
     prob = stacked(sigmoid(home_ref[...] + facts_ref[slots, :]), 2)
     prob = taken(
         summed(dot_nn(prob, rank_hits_ref[...]), CHIPS), places(place_ref)[0] - other * CHIPS
     )
     code = code_ref[...]
-    residual = (sigmoid(own_ref[...]) - ((code >> LABEL_BIT) & 1).astype(f32)) * (
+    mine = hits((code >> 7) & (DIM_ROWS - 1), DIM_ROWS)
+    score = summed(dot_nn(dims, low_ref[...]), DIM_ROWS)
+    score = own_ref[...] + jnp.sum(jnp.where(mine, score, 0.0), 0, keepdims=True)
+    residual = (sigmoid(score) - ((code >> LABEL_BIT) & 1).astype(f32)) * (
         code >> VALID_BIT
     ).astype(f32)
-    terms = split3(residual)[:2]
-    for chip in range(CHIPS):
-        cut = slice(chip * LANES, (chip + 1) * LANES)
-        mine = hits((code[chip : chip + 1] >> 7) & (DIM_ROWS - 1), DIM_ROWS)
-        for part, value in enumerate(terms):
-            left_ref[part * DIM_ROWS : (part + 1) * DIM_ROWS, cut] = jnp.where(
-                mine, value[chip : chip + 1], 0.0
-            ).astype(bf16)
+    for part, value in enumerate(split3(residual)[:2]):
+        left_ref[part * DIM_ROWS : (part + 1) * DIM_ROWS, :] = jnp.where(mine, value, 0.0).astype(
+            bf16
+        )
     return prob, summed(dot_nt(left_ref[...], low_ref[...]), DIM_ROWS)
 
 
-def same_core_kernel(
+def same_side_kernel(
     recv_ref,
     dims_ref,
     facts_ref,
@@ -312,8 +312,8 @@
 
 HALF_SCRATCH = [
     pltpu.VMEM((CHIPS, LANES), f32),
-    pltpu.VMEM((CHIPS, LANES), f32),
-    pltpu.VMEM((CHIPS, LANES), jnp.int32),
+    pltpu.VMEM((1, CHIPS * LANES), f32),
+    pltpu.VMEM((1, CHIPS * LANES), jnp.int32),
     pltpu.VMEM((LANES, CHIPS * LANES), bf16),
     pltpu.VMEM((2 * DIM_ROWS, CHIPS * LANES), bf16),
 ]
@@ -347,7 +347,7 @@
     labels = labels.reshape(1, FACTS_HERE)
     fact_weight = fact_weight.reshape(1, LANES)
     dim_weight = dim_weight.reshape(1, LANES)
-    core = (lax.axis_index("rows") & 1).reshape(1)
+    side = side_of(lax.axis_index("rows")).reshape(1)
     partial, place, meta, rank_hits = call(
         prepare_kernel,
         [
@@ -365,7 +365,7 @@
         [pl.BlockSpec(memory_space=pltpu.SMEM)]
         + [pl.BlockSpec(memory_space=pltpu.HBM)] * 7,
     )(
-        core,
+        side,
         *[
             pltpu.with_memory_space_constraint(array, pltpu.HBM)
             for array in (
@@ -390,11 +390,11 @@
         [pltpu.VMEM((3 * OWNERS, FACTS_HERE), bf16)],
     )(partial, place, meta, rank_hits)
     blocks = exchange(
-        blocks, "rows", [[2 * chip + core for chip in range(CHIPS)] for core in range(2)]
+        blocks, "rows", [[i for i in range(OWNERS) if side_of(i) == side] for side in range(2)]
     )
     other_blocks = lax.ppermute(blocks, "rows", [(i, i ^ 1) for i in range(OWNERS)])
     prob_half, sums_half, row_hits = call(
-        same_core_kernel,
+        same_side_kernel,
         [
             pltpu.VMEM((1, FACTS_HERE), f32),
             pltpu.VMEM((DIM_ROWS, LANES), f32),

time: 53.7 us -> 53.4 us (level)
  starting transfers between devices: 3.96 us -> 0.01 us
  blocking collectives: 43 us -> 46.4 us
    ppermute x1, starting transfers between devices: 3.96 us -> 0.01 us  [shards(): lax.ppermute(blocks, 'rows', [(i, i ^ 1) for i in range(OWNERS)])]
    all_to_all x3, blocking collectives: 43 us -> 46.4 us  [exchange(): lax.all_to_all(value, axis, split_axis=0, concat_axis=0, tiled=True, axis...]
where the time goes in v6:
time: 53.4 us; the launch traced here: 53.1 us
  blocking collectives  46.4 us (87%)
  Pallas kernels  5.5 us (10%)
  between operations  0.71 us (1%)
    all_to_all x3, blocking collectives, exchange(): lax.all_to_all(value, axis, split_axis=0, concat_axis=0, tiled=True, axis...  46.4 us
    pallas_call x1, Pallas kernels, shards(): call(prepare_kernel, [pltpu.VMEM((PEERS, SCORE_ROWS, LANES), f32), pltpu....  2.15 us
    pallas_call x1, Pallas kernels, shards(): call(grads_kernel, [pltpu.VMEM((OWNERS, 2, LANES), f32), jax.ShapeDtypeSt...  1.36 us
    pallas_call x1, Pallas kernels, shards(): call(same_side_kernel, [pltpu.VMEM((1, FACTS_HERE), f32), pltpu.VMEM((DIM...  1.12 us
  transfers between devices with their start and end apart: 1, of which 1 were waited for; matrix products, arithmetic and copies ran while one was open for 0% of the time, Pallas kernels for 2%

profile of v6, /device:TPU:1, one launch (start us, length us, event | category | flops | bytes accessed | tf_op | source)
XLA Modules:
  0.0 53.1 jit_solution(15051053285174369768)
XLA Ops:
  0.6 2.2 %prepare_kernel.1 = (f32[8,48,128]{2,1,0:T(8,128)S(1)}, s32[1,2048]{1,0:T(1,128)S(1)}, f32[32,128]{1,0:T(8,128)S(1)}, bf16[128,2048]{1,0:T(8,128)(2,1)S(1)}) custom-call(s32[1]{0:T(128)} %bitcast.side_ref, s32[1,2048]{1,0:T(1,128)} %bitcast.13, s32[1,2048]{1,0:T(1,128)} %bitcast.14, s32[1,2048]{1,0:T(1,128)} %bitcast.15, bf16[2048,128]{1,0:T(8,128)(2,1)} %fact_ref.1, ...), custom_call_target="tpu_custom_call" | custom-call | tf_op jit(solution)/shard_map/prepare_kernel/pallas_call | solution.py:351
  2.8 17.6 %all_to_all.15.recv_ref = f32[8,48,128]{2,1,0:T(8,128)S(1)} all-to-all(f32[8,48,128]{2,1,0:T(8,128)S(1)} %get-tuple-element.17), channel_id=1, replica_groups=mesh['rows'=32,'feat'=8] {'feat'}, dimensions={0} | all-to-all | bytes 393216 | tf_op jit(solution)/shard_map/all_to_all | solution.py:339
  20.4 0.3 pack_kernel.1
  20.7 17.3 %all_to_all.16.recv_ref = f32[16,36,128]{2,1,0:T(8,128)S(1)} all-to-all(f32[16,36,128]{2,1,0:T(8,128)S(1)} %get-tuple-element.21), channel_id=1, replica_groups={{0,16,40,56,64,80,104,120,128,144,168,184,192,208,232,248},{8,24,32,48,..., dimensions={0} | all-to-all | bytes 589824 | tf_op jit(solution)/shard_map/all_to_all | solution.py:339
  38.1 0.0 collective-permute-start
  38.1 0.0 copy-start
  38.1 0.0 copy-start.1
  38.1 1.1 %same_side_kernel.1 = (f32[1,2048]{1,0:T(1,128)S(1)}, f32[32,128]{1,0:T(8,128)S(1)}, bf16[128,2048]{1,0:T(8,128)(2,1)S(1)}) custom-call(f32[16,36,128]{2,1,0:T(8,128)S(1)} %all_to_all.16.recv_ref, f32[32,128]{1,0:T(8,128)S(1)} %get-tuple-element.22.dims_ref, f32[32,128]{1,0:T(8,128)S(1)} %get-tuple-element.23.facts_ref, ...), custom_call_target="tpu_custom_call" | custom-call | flops 2147483648 | bytes 1048576 | tf_op jit(solution)/shard_map/same_side_kernel/pallas_call | solution.py:396
  39.2 0.5 collective-permute-done.recv_ref
  39.7 0.0 copy-done
  39.7 0.0 copy-done.1
  39.7 1.4 %grads_kernel.1 = (f32[32,2,128]{2,1,0:T(2,128)S(1)}, f32[1,2048]{1,0:T(1,128)}) custom-call(f32[16,36,128]{2,1,0:T(8,128)S(1)} %collective-permute-done.recv_ref, f32[32,128]{1,0:T(8,128)S(1)} %get-tuple-element.22.dims_ref, f32[32,128]{1,0:T(8,128)S(1)} %get-tuple-element.23.facts_ref, f32[32,128]{1,0:T(8,128)S(1)} %get-tuple-element.19.meta_ref, ...), custom_call_target="tpu_custom_call" | custom-call | tf_op jit(solution)/shard_map/grads_kernel/pallas_call | solution.py:406
  41.1 0.0 copy-start.2
  41.1 0.0 copy-start.3
  41.1 11.5 %all_to_all.17.recv_ref = f32[32,2,128]{2,1,0:T(2,128)S(1)} all-to-all(f32[32,2,128]{2,1,0:T(2,128)S(1)} %get-tuple-element.27), channel_id=1, replica_groups=mesh['rows'=32,'feat'=8] {'rows'}, dimensions={0} | all-to-all | bytes 65536 | tf_op jit(solution)/shard_map/all_to_all | solution.py:339
  52.6 0.0 copy-done.2
  52.6 0.0 copy-done.3
  52.6 0.6 %update_kernel.1 = (f32[1,128]{1,0:T(1,128)}, f32[1,128]{1,0:T(1,128)}) custom-call(f32[32,2,128]{2,1,0:T(2,128)S(1)} %all_to_all.17.recv_ref, f32[1,128]{1,0:T(1,128)S(1)} %bitcast.10, f32[1,128]{1,0:T(1,128)S(1)} %bitcast.12), custom_call_target="tpu_custom_call" | custom-call | tf_op jit(solution)/shard_map/update_kernel/pallas_call | solution.py:427
Async XLA Ops:
  38.1 1.6 %collective-permute-start = (f32[16,36,128]{2,1,0:T(8,128)S(1)}, f32[16,36,128]{2,1,0:T(8,128)S(1)}, u32[]{:S(2)}, u32[]{:S(2)}) collective-permute-start(f32[16,36,128]{2,1,0:T(8,128)S(1)} %all_to_all.16.recv_ref), channel_id=1, source_target_pairs={{0,8},{8,0},{16,24},{24,16},{32,40},{40,32},{48,56},{56,48},{64,72... | collective-permute-start | bytes 884744 | tf_op jit(solution)/shard_map/ppermute | solution.py:395
  38.1 1.6 %copy-start = (bf16[4096,128]{1,0:T(8,128)(2,1)S(1)}, bf16[4096,128]{1,0:T(8,128)(2,1)}, u32[]{:S(2)}) copy-start(bf16[4096,128]{1,0:T(8,128)(2,1)} %dim_ref.1) | copy-start | bytes 3145732
  38.1 1.6 %copy-start.1 = (bf16[2048,128]{1,0:T(8,128)(2,1)S(1)}, bf16[2048,128]{1,0:T(8,128)(2,1)}, u32[]{:S(2)}) copy-start(bf16[2048,128]{1,0:T(8,128)(2,1)} %fact_ref.1) | copy-start | bytes 1572868
  41.1 11.5 %copy-start.2 = (f32[128]{0:T(128)S(1)}, f32[128]{0:T(128)}, u32[]{:S(2)}) copy-start(f32[128]{0:T(128)} %param.9) | copy-start | bytes 1540
  41.1 11.5 %copy-start.3 = (f32[128]{0:T(128)S(1)}, f32[128]{0:T(128)}, u32[]{:S(2)}) copy-start(f32[128]{0:T(128)} %param.10) | copy-start | bytes 1540

commit v7 on v6

--- a/solution.py
+++ b/solution.py
@@ -60,6 +60,18 @@
     return (row ^ (row >> 2)) & 1
 
 
+def place_of(row):
+    return (((row >> 1) & 3) << 2) + (row >> 3)
+
+
+FEAT_ORDER = [7, 3, 5, 1, 6, 2, 4, 0]
+SIDES = [
+    sorted((row for row in range(OWNERS) if side_of(row) == side), key=place_of)
+    for side in range(2)
+]
+CORE_ORDER = sorted(range(OWNERS), key=lambda row: row & 1)
+
+
 def place_facts(side, bucket, index, label, place_ref, meta_ref, rank_hits_ref):
     width = 2 * LANES
     chunks = FACTS_HERE // width
@@ -69,7 +81,7 @@
         1.0,
         0.0,
     ).astype(bf16)
-    owner = (bucket >> 1) + (side_of(bucket) ^ side) * CHIPS
+    owner = place_of(bucket) + (side_of(bucket) ^ side) * CHIPS
     owner_hits = onehot(owner, OWNERS)
     stack = jnp.concatenate(
         [owner_hits[:, c * width : (c + 1) * width] for c in range(chunks)], 0
@@ -379,7 +391,7 @@
             )
         ],
     )
-    partial = exchange(partial, "feat")
+    partial = exchange(partial, "feat", [FEAT_ORDER])
     blocks, dims, facts = call(
         pack_kernel,
         [
@@ -390,7 +402,7 @@
         [pltpu.VMEM((3 * OWNERS, FACTS_HERE), bf16)],
     )(partial, place, meta, rank_hits)
     blocks = exchange(
-        blocks, "rows", [[i for i in range(OWNERS) if side_of(i) == side] for side in range(2)]
+        blocks, "rows", SIDES
     )
     other_blocks = lax.ppermute(blocks, "rows", [(i, i ^ 1) for i in range(OWNERS)])
     prob_half, sums_half, row_hits = call(
@@ -423,7 +435,7 @@
         fact_table,
         dim_table,
     )
-    grads = exchange(grads, "rows")
+    grads = exchange(grads, "rows", [CORE_ORDER])
     new_fact, new_dim = call(update_kernel, [jax.ShapeDtypeStruct((1, LANES), f32)] * 2)(
         grads, fact_weight, dim_weight
     )

time: 53.4 us -> 49.4 us (0.925)
  blocking collectives: 46.4 us -> 42.4 us
    all_to_all x3, blocking collectives: 46.4 us -> 42.4 us  [exchange(): lax.all_to_all(value, axis, split_axis=0, concat_axis=0, tiled=True, axis...]
where the time goes in v7:
time: 49.4 us; the launch traced here: 49.1 us
  blocking collectives  42.4 us (86%)
  Pallas kernels  5.5 us (11%)
  between operations  0.71 us (1%)
    all_to_all x3, blocking collectives, exchange(): lax.all_to_all(value, axis, split_axis=0, concat_axis=0, tiled=True, axis...  42.4 us
    pallas_call x1, Pallas kernels, shards(): call(prepare_kernel, [pltpu.VMEM((PEERS, SCORE_ROWS, LANES), f32), pltpu....  2.15 us
    pallas_call x1, Pallas kernels, shards(): call(grads_kernel, [pltpu.VMEM((OWNERS, 2, LANES), f32), jax.ShapeDtypeSt...  1.36 us
    pallas_call x1, Pallas kernels, shards(): call(same_side_kernel, [pltpu.VMEM((1, FACTS_HERE), f32), pltpu.VMEM((DIM...  1.12 us
  transfers between devices with their start and end apart: 1, of which 1 were waited for; matrix products, arithmetic and copies ran while one was open for 0% of the time, Pallas kernels for 2%

profile of v7, /device:TPU:1, one launch (start us, length us, event | category | flops | bytes accessed | tf_op | source)
XLA Modules:
  0.0 49.1 jit_solution(20301036031940582)
XLA Ops:
  0.6 2.2 %prepare_kernel.1 = (f32[8,48,128]{2,1,0:T(8,128)S(1)}, s32[1,2048]{1,0:T(1,128)S(1)}, f32[32,128]{1,0:T(8,128)S(1)}, bf16[128,2048]{1,0:T(8,128)(2,1)S(1)}) custom-call(s32[1]{0:T(128)} %bitcast.side_ref, s32[1,2048]{1,0:T(1,128)} %bitcast.13, s32[1,2048]{1,0:T(1,128)} %bitcast.14, s32[1,2048]{1,0:T(1,128)} %bitcast.15, bf16[2048,128]{1,0:T(8,128)(2,1)} %fact_ref.1, ...), custom_call_target="tpu_custom_call" | custom-call | tf_op jit(solution)/shard_map/prepare_kernel/pallas_call | solution.py:363
  2.8 14.2 %all_to_all.15.recv_ref = f32[8,48,128]{2,1,0:T(8,128)S(1)} all-to-all(f32[8,48,128]{2,1,0:T(8,128)S(1)} %get-tuple-element.17), channel_id=1, replica_groups={{7,3,5,1,6,2,4,0},{15,11,13,9,14,10,12,8},{23,19,21,17,22,18,20,16},{31..., dimensions={0} | all-to-all | bytes 393216 | tf_op jit(solution)/shard_map/all_to_all | solution.py:351
  17.0 0.3 pack_kernel.1
  17.3 17.4 %all_to_all.16.recv_ref = f32[16,36,128]{2,1,0:T(8,128)S(1)} all-to-all(f32[16,36,128]{2,1,0:T(8,128)S(1)} %get-tuple-element.21), channel_id=1, replica_groups={{0,64,128,192,16,80,144,208,40,104,168,232,56,120,184,248},{8,72,136,20..., dimensions={0} | all-to-all | bytes 589824 | tf_op jit(solution)/shard_map/all_to_all | solution.py:351
  34.8 0.0 collective-permute-start
  34.8 0.0 copy-start
  34.8 0.0 copy-start.1
  34.8 1.1 %same_side_kernel.1 = (f32[1,2048]{1,0:T(1,128)S(1)}, f32[32,128]{1,0:T(8,128)S(1)}, bf16[128,2048]{1,0:T(8,128)(2,1)S(1)}) custom-call(f32[16,36,128]{2,1,0:T(8,128)S(1)} %all_to_all.16.recv_ref, f32[32,128]{1,0:T(8,128)S(1)} %get-tuple-element.22.dims_ref, f32[32,128]{1,0:T(8,128)S(1)} %get-tuple-element.23.facts_ref, ...), custom_call_target="tpu_custom_call" | custom-call | flops 2147483648 | bytes 1048576 | tf_op jit(solution)/shard_map/same_side_kernel/pallas_call | solution.py:408
  35.9 0.5 collective-permute-done.recv_ref
  36.4 0.0 copy-done
  36.4 0.0 copy-done.1
  36.4 1.4 %grads_kernel.1 = (f32[32,2,128]{2,1,0:T(2,128)S(1)}, f32[1,2048]{1,0:T(1,128)}) custom-call(f32[16,36,128]{2,1,0:T(8,128)S(1)} %collective-permute-done.recv_ref, f32[32,128]{1,0:T(8,128)S(1)} %get-tuple-element.22.dims_ref, f32[32,128]{1,0:T(8,128)S(1)} %get-tuple-element.23.facts_ref, f32[32,128]{1,0:T(8,128)S(1)} %get-tuple-element.19.meta_ref, ...), custom_call_target="tpu_custom_call" | custom-call | tf_op jit(solution)/shard_map/grads_kernel/pallas_call | solution.py:418
  37.8 0.0 copy-start.2
  37.8 0.0 copy-start.3
  37.8 10.8 %all_to_all.17.recv_ref = f32[32,2,128]{2,1,0:T(2,128)S(1)} all-to-all(f32[32,2,128]{2,1,0:T(2,128)S(1)} %get-tuple-element.27), channel_id=1, replica_groups={{0,16,32,48,64,80,96,112,128,144,160,176,192,208,224,240,8,24,40,56,72,..., dimensions={0} | all-to-all | bytes 65536 | tf_op jit(solution)/shard_map/all_to_all | solution.py:351
  48.6 0.0 copy-done.2
  48.6 0.0 copy-done.3
  48.6 0.6 %update_kernel.1 = (f32[1,128]{1,0:T(1,128)}, f32[1,128]{1,0:T(1,128)}) custom-call(f32[32,2,128]{2,1,0:T(2,128)S(1)} %all_to_all.17.recv_ref, f32[1,128]{1,0:T(1,128)S(1)} %bitcast.10, f32[1,128]{1,0:T(1,128)S(1)} %bitcast.12), custom_call_target="tpu_custom_call" | custom-call | tf_op jit(solution)/shard_map/update_kernel/pallas_call | solution.py:439
Async XLA Ops:
  34.8 1.6 %collective-permute-start = (f32[16,36,128]{2,1,0:T(8,128)S(1)}, f32[16,36,128]{2,1,0:T(8,128)S(1)}, u32[]{:S(2)}, u32[]{:S(2)}) collective-permute-start(f32[16,36,128]{2,1,0:T(8,128)S(1)} %all_to_all.16.recv_ref), channel_id=1, source_target_pairs={{0,8},{8,0},{16,24},{24,16},{32,40},{40,32},{48,56},{56,48},{64,72... | collective-permute-start | bytes 884744 | tf_op jit(solution)/shard_map/ppermute | solution.py:407
  34.8 1.6 %copy-start = (bf16[4096,128]{1,0:T(8,128)(2,1)S(1)}, bf16[4096,128]{1,0:T(8,128)(2,1)}, u32[]{:S(2)}) copy-start(bf16[4096,128]{1,0:T(8,128)(2,1)} %dim_ref.1) | copy-start | bytes 3145732
  34.8 1.6 %copy-start.1 = (bf16[2048,128]{1,0:T(8,128)(2,1)S(1)}, bf16[2048,128]{1,0:T(8,128)(2,1)}, u32[]{:S(2)}) copy-start(bf16[2048,128]{1,0:T(8,128)(2,1)} %fact_ref.1) | copy-start | bytes 1572868
  37.8 10.8 %copy-start.2 = (f32[128]{0:T(128)S(1)}, f32[128]{0:T(128)}, u32[]{:S(2)}) copy-start(f32[128]{0:T(128)} %param.9) | copy-start | bytes 1540
  37.8 10.8 %copy-start.3 = (f32[128]{0:T(128)S(1)}, f32[128]{0:T(128)}, u32[]{:S(2)}) copy-start(f32[128]{0:T(128)} %param.10) | copy-start | bytes 1540

commit v8 on v7

--- a/solution.py
+++ b/solution.py
@@ -61,15 +61,15 @@
 
 
 def place_of(row):
-    return (((row >> 1) & 3) << 2) + (row >> 3)
-
-
-FEAT_ORDER = [7, 3, 5, 1, 6, 2, 4, 0]
+    return CHIPS - 1 - (((row >> 1) & 3) << 2) - (row >> 3)
+
+
+FEAT_ORDER = [7, 3, 6, 2, 5, 1, 4, 0]
 SIDES = [
     sorted((row for row in range(OWNERS) if side_of(row) == side), key=place_of)
     for side in range(2)
 ]
-CORE_ORDER = sorted(range(OWNERS), key=lambda row: row & 1)
+ROW_ORDER = list(range(OWNERS))[::-1]
 
 
 def place_facts(side, bucket, index, label, place_ref, meta_ref, rank_hits_ref):
@@ -435,7 +435,7 @@
         fact_table,
         dim_table,
     )
-    grads = exchange(grads, "rows", [CORE_ORDER])
+    grads = exchange(grads, "rows", [ROW_ORDER])
     new_fact, new_dim = call(update_kernel, [jax.ShapeDtypeStruct((1, LANES), f32)] * 2)(
         grads, fact_weight, dim_weight
     )

time: 49.4 us -> 47.6 us (0.964)
  blocking collectives: 42.4 us -> 40.7 us
    all_to_all x3, blocking collectives: 42.4 us -> 40.7 us  [exchange(): lax.all_to_all(value, axis, split_axis=0, concat_axis=0, tiled=True, axis...]
where the time goes in v8:
time: 47.6 us; the launch traced here: 47.4 us
  blocking collectives  40.7 us (86%)
  Pallas kernels  5.5 us (12%)
  between operations  0.71 us (1%)
    all_to_all x3, blocking collectives, exchange(): lax.all_to_all(value, axis, split_axis=0, concat_axis=0, tiled=True, axis...  40.7 us
    pallas_call x1, Pallas kernels, shards(): call(prepare_kernel, [pltpu.VMEM((PEERS, SCORE_ROWS, LANES), f32), pltpu....  2.15 us
    pallas_call x1, Pallas kernels, shards(): call(grads_kernel, [pltpu.VMEM((OWNERS, 2, LANES), f32), jax.ShapeDtypeSt...  1.36 us
    pallas_call x1, Pallas kernels, shards(): call(same_side_kernel, [pltpu.VMEM((1, FACTS_HERE), f32), pltpu.VMEM((DIM...  1.12 us
  transfers between devices with their start and end apart: 1, of which 1 were waited for; matrix products, arithmetic and copies ran while one was open for 0% of the time, Pallas kernels for 2%

profile of v8, /device:TPU:1, one launch (start us, length us, event | category | flops | bytes accessed | tf_op | source)
XLA Modules:
  0.0 47.4 jit_solution(12012021827694082574)
XLA Ops:
  0.6 2.2 %prepare_kernel.1 = (f32[8,48,128]{2,1,0:T(8,128)S(1)}, s32[1,2048]{1,0:T(1,128)S(1)}, f32[32,128]{1,0:T(8,128)S(1)}, bf16[128,2048]{1,0:T(8,128)(2,1)S(1)}) custom-call(s32[1]{0:T(128)} %bitcast.side_ref, s32[1,2048]{1,0:T(1,128)} %bitcast.13, s32[1,2048]{1,0:T(1,128)} %bitcast.14, s32[1,2048]{1,0:T(1,128)} %bitcast.15, bf16[2048,128]{1,0:T(8,128)(2,1)} %fact_ref.1, ...), custom_call_target="tpu_custom_call" | custom-call | tf_op jit(solution)/shard_map/prepare_kernel/pallas_call | solution.py:363
  2.8 14.2 %all_to_all.15.recv_ref = f32[8,48,128]{2,1,0:T(8,128)S(1)} all-to-all(f32[8,48,128]{2,1,0:T(8,128)S(1)} %get-tuple-element.17), channel_id=1, replica_groups={{7,3,6,2,5,1,4,0},{15,11,14,10,13,9,12,8},{23,19,22,18,21,17,20,16},{31..., dimensions={0} | all-to-all | bytes 393216 | tf_op jit(solution)/shard_map/all_to_all | solution.py:351
  17.0 0.3 pack_kernel.1
  17.3 16.0 %all_to_all.16.recv_ref = f32[16,36,128]{2,1,0:T(8,128)S(1)} all-to-all(f32[16,36,128]{2,1,0:T(8,128)S(1)} %get-tuple-element.21), channel_id=1, replica_groups={{248,184,120,56,232,168,104,40,208,144,80,16,192,128,64,0},{240,176,112..., dimensions={0} | all-to-all | bytes 589824 | tf_op jit(solution)/shard_map/all_to_all | solution.py:351
  33.3 0.3 collective-permute-start
  33.6 0.0 copy-start
  33.6 0.0 copy-start.1
  33.6 1.1 %same_side_kernel.1 = (f32[1,2048]{1,0:T(1,128)S(1)}, f32[32,128]{1,0:T(8,128)S(1)}, bf16[128,2048]{1,0:T(8,128)(2,1)S(1)}) custom-call(f32[16,36,128]{2,1,0:T(8,128)S(1)} %all_to_all.16.recv_ref, f32[32,128]{1,0:T(8,128)S(1)} %get-tuple-element.22.dims_ref, f32[32,128]{1,0:T(8,128)S(1)} %get-tuple-element.23.facts_ref, ...), custom_call_target="tpu_custom_call" | custom-call | flops 2147483648 | bytes 1048576 | tf_op jit(solution)/shard_map/same_side_kernel/pallas_call | solution.py:408
  34.8 0.2 collective-permute-done.recv_ref
  35.0 0.0 copy-done
  35.0 0.0 copy-done.1
  35.0 1.4 %grads_kernel.1 = (f32[32,2,128]{2,1,0:T(2,128)S(1)}, f32[1,2048]{1,0:T(1,128)}) custom-call(f32[16,36,128]{2,1,0:T(8,128)S(1)} %collective-permute-done.recv_ref, f32[32,128]{1,0:T(8,128)S(1)} %get-tuple-element.22.dims_ref, f32[32,128]{1,0:T(8,128)S(1)} %get-tuple-element.23.facts_ref, f32[32,128]{1,0:T(8,128)S(1)} %get-tuple-element.19.meta_ref, ...), custom_call_target="tpu_custom_call" | custom-call | tf_op jit(solution)/shard_map/grads_kernel/pallas_call | solution.py:418
  36.4 0.0 copy-start.2
  36.4 0.0 copy-start.3
  36.4 10.4 %all_to_all.17.recv_ref = f32[32,2,128]{2,1,0:T(2,128)S(1)} all-to-all(f32[32,2,128]{2,1,0:T(2,128)S(1)} %get-tuple-element.27), channel_id=1, replica_groups={{248,240,232,224,216,208,200,192,184,176,168,160,152,144,136,128,120,11..., dimensions={0} | all-to-all | bytes 65536 | tf_op jit(solution)/shard_map/all_to_all | solution.py:351
  46.8 0.0 copy-done.2
  46.8 0.0 copy-done.3
  46.8 0.6 %update_kernel.1 = (f32[1,128]{1,0:T(1,128)}, f32[1,128]{1,0:T(1,128)}) custom-call(f32[32,2,128]{2,1,0:T(2,128)S(1)} %all_to_all.17.recv_ref, f32[1,128]{1,0:T(1,128)S(1)} %bitcast.10, f32[1,128]{1,0:T(1,128)S(1)} %bitcast.12), custom_call_target="tpu_custom_call" | custom-call | tf_op jit(solution)/shard_map/update_kernel/pallas_call | solution.py:439
Async XLA Ops:
  33.3 1.6 %collective-permute-start = (f32[16,36,128]{2,1,0:T(8,128)S(1)}, f32[16,36,128]{2,1,0:T(8,128)S(1)}, u32[]{:S(2)}, u32[]{:S(2)}) collective-permute-start(f32[16,36,128]{2,1,0:T(8,128)S(1)} %all_to_all.16.recv_ref), channel_id=1, source_target_pairs={{0,8},{8,0},{16,24},{24,16},{32,40},{40,32},{48,56},{56,48},{64,72... | collective-permute-start | bytes 884744 | tf_op jit(solution)/shard_map/ppermute | solution.py:407
  33.6 1.3 %copy-start = (bf16[4096,128]{1,0:T(8,128)(2,1)S(1)}, bf16[4096,128]{1,0:T(8,128)(2,1)}, u32[]{:S(2)}) copy-start(bf16[4096,128]{1,0:T(8,128)(2,1)} %dim_ref.1) | copy-start | bytes 3145732
  33.6 1.4 %copy-start.1 = (bf16[2048,128]{1,0:T(8,128)(2,1)S(1)}, bf16[2048,128]{1,0:T(8,128)(2,1)}, u32[]{:S(2)}) copy-start(bf16[2048,128]{1,0:T(8,128)(2,1)} %fact_ref.1) | copy-start | bytes 1572868
  36.4 10.5 %copy-start.2 = (f32[128]{0:T(128)S(1)}, f32[128]{0:T(128)}, u32[]{:S(2)}) copy-start(f32[128]{0:T(128)} %param.9) | copy-start | bytes 1540
  36.4 10.5 %copy-start.3 = (f32[128]{0:T(128)S(1)}, f32[128]{0:T(128)}, u32[]{:S(2)}) copy-start(f32[128]{0:T(128)} %param.10) | copy-start | bytes 1540

commit v9 on v8

--- a/solution.py
+++ b/solution.py
@@ -69,7 +69,10 @@
     sorted((row for row in range(OWNERS) if side_of(row) == side), key=place_of)
     for side in range(2)
 ]
-ROW_ORDER = list(range(OWNERS))[::-1]
+FAR = [0, 1, 3, 2]
+ROW_ORDER = sorted(
+    range(OWNERS), key=lambda row: (-FAR[row >> 3] - FAR[(row >> 1) & 3], -row)
+)
 
 
 def place_facts(side, bucket, index, label, place_ref, meta_ref, rank_hits_ref):

time: 47.6 us -> 46.6 us (0.979)
  blocking collectives: 40.7 us -> 39.6 us
    all_to_all x3, blocking collectives: 40.7 us -> 39.6 us  [exchange(): lax.all_to_all(value, axis, split_axis=0, concat_axis=0, tiled=True, axis...]
where the time goes in v9:
time: 46.6 us; the launch traced here: 46.4 us
  blocking collectives  39.6 us (85%)
  Pallas kernels  5.5 us (12%)
  between operations  0.71 us (2%)
    all_to_all x3, blocking collectives, exchange(): lax.all_to_all(value, axis, split_axis=0, concat_axis=0, tiled=True, axis...  39.6 us
    pallas_call x1, Pallas kernels, shards(): call(prepare_kernel, [pltpu.VMEM((PEERS, SCORE_ROWS, LANES), f32), pltpu....  2.15 us
    pallas_call x1, Pallas kernels, shards(): call(grads_kernel, [pltpu.VMEM((OWNERS, 2, LANES), f32), jax.ShapeDtypeSt...  1.36 us
    pallas_call x1, Pallas kernels, shards(): call(same_side_kernel, [pltpu.VMEM((1, FACTS_HERE), f32), pltpu.VMEM((DIM...  1.12 us
  transfers between devices with their start and end apart: 1, of which 1 were waited for; matrix products, arithmetic and copies ran while one was open for 0% of the time, Pallas kernels for 2%

profile of v9, /device:TPU:1, one launch (start us, length us, event | category | flops | bytes accessed | tf_op | source)
XLA Modules:
  0.0 46.4 jit_solution(15718444485538927736)
XLA Ops:
  0.6 2.2 %prepare_kernel.1 = (f32[8,48,128]{2,1,0:T(8,128)S(1)}, s32[1,2048]{1,0:T(1,128)S(1)}, f32[32,128]{1,0:T(8,128)S(1)}, bf16[128,2048]{1,0:T(8,128)(2,1)S(1)}) custom-call(s32[1]{0:T(128)} %bitcast.side_ref, s32[1,2048]{1,0:T(1,128)} %bitcast.13, s32[1,2048]{1,0:T(1,128)} %bitcast.14, s32[1,2048]{1,0:T(1,128)} %bitcast.15, bf16[2048,128]{1,0:T(8,128)(2,1)} %fact_ref.1, ...), custom_call_target="tpu_custom_call" | custom-call | tf_op jit(solution)/shard_map/prepare_kernel/pallas_call | solution.py:366
  2.8 14.2 %all_to_all.15.recv_ref = f32[8,48,128]{2,1,0:T(8,128)S(1)} all-to-all(f32[8,48,128]{2,1,0:T(8,128)S(1)} %get-tuple-element.17), channel_id=1, replica_groups={{7,3,6,2,5,1,4,0},{15,11,14,10,13,9,12,8},{23,19,22,18,21,17,20,16},{31..., dimensions={0} | all-to-all | bytes 393216 | tf_op jit(solution)/shard_map/all_to_all | solution.py:354
  17.0 0.3 pack_kernel.1
  17.3 16.0 %all_to_all.16.recv_ref = f32[16,36,128]{2,1,0:T(8,128)S(1)} all-to-all(f32[16,36,128]{2,1,0:T(8,128)S(1)} %get-tuple-element.21), channel_id=1, replica_groups={{248,184,120,56,232,168,104,40,208,144,80,16,192,128,64,0},{240,176,112..., dimensions={0} | all-to-all | bytes 589824 | tf_op jit(solution)/shard_map/all_to_all | solution.py:354
  33.3 0.3 collective-permute-start
  33.6 0.0 copy-start
  33.6 0.0 copy-start.1
  33.6 1.1 %same_side_kernel.1 = (f32[1,2048]{1,0:T(1,128)S(1)}, f32[32,128]{1,0:T(8,128)S(1)}, bf16[128,2048]{1,0:T(8,128)(2,1)S(1)}) custom-call(f32[16,36,128]{2,1,0:T(8,128)S(1)} %all_to_all.16.recv_ref, f32[32,128]{1,0:T(8,128)S(1)} %get-tuple-element.22.dims_ref, f32[32,128]{1,0:T(8,128)S(1)} %get-tuple-element.23.facts_ref, ...), custom_call_target="tpu_custom_call" | custom-call | flops 2147483648 | bytes 1048576 | tf_op jit(solution)/shard_map/same_side_kernel/pallas_call | solution.py:411
  34.8 0.2 collective-permute-done.recv_ref
  35.0 0.0 copy-done
  35.0 0.0 copy-done.1
  35.0 1.4 %grads_kernel.1 = (f32[32,2,128]{2,1,0:T(2,128)S(1)}, f32[1,2048]{1,0:T(1,128)}) custom-call(f32[16,36,128]{2,1,0:T(8,128)S(1)} %collective-permute-done.recv_ref, f32[32,128]{1,0:T(8,128)S(1)} %get-tuple-element.22.dims_ref, f32[32,128]{1,0:T(8,128)S(1)} %get-tuple-element.23.facts_ref, f32[32,128]{1,0:T(8,128)S(1)} %get-tuple-element.19.meta_ref, ...), custom_call_target="tpu_custom_call" | custom-call | tf_op jit(solution)/shard_map/grads_kernel/pallas_call | solution.py:421
  36.4 0.0 copy-start.2
  36.4 0.0 copy-start.3
  36.4 9.4 %all_to_all.17.recv_ref = f32[32,2,128]{2,1,0:T(2,128)S(1)} all-to-all(f32[32,2,128]{2,1,0:T(2,128)S(1)} %get-tuple-element.27), channel_id=1, replica_groups={{168,160,232,224,184,176,248,240,152,144,104,96,216,208,136,128,120,112..., dimensions={0} | all-to-all | bytes 65536 | tf_op jit(solution)/shard_map/all_to_all | solution.py:354
  45.8 0.0 copy-done.2
  45.8 0.0 copy-done.3
  45.8 0.6 %update_kernel.1 = (f32[1,128]{1,0:T(1,128)}, f32[1,128]{1,0:T(1,128)}) custom-call(f32[32,2,128]{2,1,0:T(2,128)S(1)} %all_to_all.17.recv_ref, f32[1,128]{1,0:T(1,128)S(1)} %bitcast.10, f32[1,128]{1,0:T(1,128)S(1)} %bitcast.12), custom_call_target="tpu_custom_call" | custom-call | tf_op jit(solution)/shard_map/update_kernel/pallas_call | solution.py:442
Async XLA Ops:
  33.3 1.6 %collective-permute-start = (f32[16,36,128]{2,1,0:T(8,128)S(1)}, f32[16,36,128]{2,1,0:T(8,128)S(1)}, u32[]{:S(2)}, u32[]{:S(2)}) collective-permute-start(f32[16,36,128]{2,1,0:T(8,128)S(1)} %all_to_all.16.recv_ref), channel_id=1, source_target_pairs={{0,8},{8,0},{16,24},{24,16},{32,40},{40,32},{48,56},{56,48},{64,72... | collective-permute-start | bytes 884744 | tf_op jit(solution)/shard_map/ppermute | solution.py:410
  33.6 1.3 %copy-start = (bf16[4096,128]{1,0:T(8,128)(2,1)S(1)}, bf16[4096,128]{1,0:T(8,128)(2,1)}, u32[]{:S(2)}) copy-start(bf16[4096,128]{1,0:T(8,128)(2,1)} %dim_ref.1) | copy-start | bytes 3145732
  33.6 1.4 %copy-start.1 = (bf16[2048,128]{1,0:T(8,128)(2,1)S(1)}, bf16[2048,128]{1,0:T(8,128)(2,1)}, u32[]{:S(2)}) copy-start(bf16[2048,128]{1,0:T(8,128)(2,1)} %fact_ref.1) | copy-start | bytes 1572868
  36.4 9.4 %copy-start.2 = (f32[128]{0:T(128)S(1)}, f32[128]{0:T(128)}, u32[]{:S(2)}) copy-start(f32[128]{0:T(128)} %param.9) | copy-start | bytes 1540
  36.4 9.4 %copy-start.3 = (f32[128]{0:T(128)S(1)}, f32[128]{0:T(128)}, u32[]{:S(2)}) copy-start(f32[128]{0:T(128)} %param.10) | copy-start | bytes 1540
